TPU v7x, 256 devices: a whole 4x4x8 slice. The times are simulated.
256 devices in a mesh: dp: 2 (over y_lo), fsdp: 16 (over z, y_hi), seq: 8 (over x, core).
Axes of the slice: x: 4, y: 4 (y_hi: 2, y_lo: 2; y = y_hi * 2 + y_lo), z: 8, core: 2. Of those that a mesh axis runs over, the one named last changes fastest.
Arguments:
- latents: bfloat16 [32, 512, 2, 3072], P(('dp', 'fsdp'), 'seq'), may hold values from -6 to 6
- noise: bfloat16 [32, 512, 2, 3072], P(('dp', 'fsdp'), 'seq'), may hold values from -12 to 12
- timesteps: int32 [32, 2], P(('dp', 'fsdp')), may hold values from 0 to 999
- ref_errors: float32 [32, 2], P(('dp', 'fsdp')), may hold values from 1.5 to 2.5
- norm_gain: float32 [3072], replicated, may hold values from 0.25 to 1.75
- w_query: bfloat16 [3072, 2048], P('fsdp', 'seq'), as said below
- w_key: bfloat16 [3072, 2048], P('fsdp', 'seq'), as said below
- w_value: bfloat16 [3072, 2048], P('fsdp', 'seq'), may hold values from -0.109375 to 0.109375
- w_out: bfloat16 [2048, 3072], P('seq', 'fsdp'), may hold values from -0.125 to 0.125
Outputs:
- grad_value: bfloat16 [3072, 2048], P(('dp', 'fsdp'), 'seq')
- grad_out: bfloat16 [2048, 3072], P('seq', ('dp', 'fsdp'))
- pair_loss: float32 [32], P(('dp', 'fsdp'))
Inputs may be any that keep to these rules, and one draw needn't show every extreme that they name: `w_query`: columns of the query projection, of order 1 / sqrt(3072). `w_key`: columns of the key projection.
All inputs are finite; a program needn't handle non-finite values.
Results may differ from a plain program's by a relative error of at most 0.025.
Values may be sent and summed in bfloat16 or wider, within the bound.
No kernel may reach another device: no remote copies, remote signals or barrier semaphores. Data moves between devices by JAX's collectives and lax.ppermute only.
A program may use at most 128 MiB of HBM per device.

v0:
```python
import math

import jax
import jax.numpy as jnp
from jax import lax
from jax.sharding import PartitionSpec as P

HD = 128
NSTEP = 1000
LOSS_SCALE = 24576


preference_beta = 2.0
norm_epsilon = 1e-06


def rms_normed(values, norm_gain):
    values = values.astype(jnp.float32)
    inverse = lax.rsqrt(jnp.mean(values * values, axis=-1, keepdims=True) + norm_epsilon)
    return (values * inverse * norm_gain).astype(jnp.bfloat16)


def body(latents, noise, timesteps, ref_errors, norm_gain, w_query, w_key, w_value, w_out):
    seq_count = lax.axis_size("seq")
    local_len = latents.shape[1]
    full_len = local_len * seq_count
    model_width = latents.shape[3]
    local_width = w_query.shape[1]
    head_count = local_width // HD
    clean32 = latents[0].astype(jnp.float32)
    noise32 = noise[0].astype(jnp.float32)
    sigma = (timesteps[0].astype(jnp.float32) + 0.5) / NSTEP
    mixing = sigma[None, :, None]
    noised = ((1.0 - mixing) * clean32 + mixing * noise32).astype(jnp.bfloat16)
    target = noise32 - clean32
    normed = rms_normed(lax.all_gather(noised, "seq", axis=0, tiled=True), norm_gain)
    query_w, key_w, value_w = (
        lax.all_gather(w_query, "fsdp", axis=0, tiled=True),
        lax.all_gather(w_key, "fsdp", axis=0, tiled=True),
        lax.all_gather(w_value, "fsdp", axis=0, tiled=True),
    )
    out_w = lax.all_gather(w_out, "fsdp", axis=1, tiled=True)
    rows = normed.reshape(full_len * 2, model_width)

    def project(weight):
        product = jnp.dot(rows, weight, preferred_element_type=jnp.float32)
        return product.astype(jnp.bfloat16).reshape(full_len, 2, head_count, HD)

    query = project(query_w)
    keys = project(key_w)
    values = project(value_w)
    scores = jnp.einsum(
        "tihd,sihd->ihts", query, keys, preferred_element_type=jnp.float32
    ) / math.sqrt(HD)
    probs = jax.nn.softmax(scores, axis=-1).astype(jnp.bfloat16)
    attended = jnp.einsum(
        "ihts,sihd->tihd", probs, values, preferred_element_type=jnp.float32
    ).astype(jnp.bfloat16)
    attended = attended.reshape(full_len, 2, local_width)
    flat_attended = attended.reshape(full_len * 2, local_width)
    predicted = lax.psum_scatter(
        jnp.dot(flat_attended, out_w, preferred_element_type=jnp.float32).astype(jnp.bfloat16),
        "seq",
        scatter_dimension=0,
        tiled=True,
    ).astype(jnp.float32)
    predicted = predicted.reshape(local_len, 2, model_width)
    differ = predicted - target
    local_sums = jnp.sum(differ * differ, axis=(0, 2))
    totals = lax.psum(local_sums, "seq")
    errors = totals / (full_len * model_width)
    residual = differ.astype(jnp.bfloat16)
    residual_full = lax.all_gather(residual, "seq", axis=0, tiled=True)
    reference_pair = ref_errors[0]
    margin = errors[0] - reference_pair[0] - (errors[1] - reference_pair[1])
    pair_loss = jax.nn.softplus(preference_beta * margin)
    weight_pair = (
        preference_beta
        * jax.nn.sigmoid(preference_beta * margin)
        * 2.0
        * LOSS_SCALE
        / (full_len * model_width)
    )
    image_scale = jnp.array([1.0, -1.0], jnp.float32) * weight_pair
    residual_rows = residual_full.reshape(full_len * 2, model_width)
    d_attended = lax.dot_general(
        residual_rows, out_w, (((1,), (1,)), ((), ())), preferred_element_type=jnp.float32
    )
    d_attended = (d_attended.reshape(full_len, 2, local_width) * image_scale[None, :, None]).astype(
        jnp.bfloat16
    )
    d_attended = d_attended.reshape(full_len, 2, head_count, HD)
    d_values = jnp.einsum(
        "ihts,tihd->sihd", probs, d_attended, preferred_element_type=jnp.float32
    ).astype(jnp.bfloat16)
    d_values = d_values.reshape(full_len * 2, local_width)
    grad_val = lax.dot_general(
        rows, d_values, (((0,), (0,)), ((), ())), preferred_element_type=jnp.float32
    )
    per_image = lax.dot_general(
        residual_full, attended, (((0,), (0,)), ((1,), (1,))), preferred_element_type=jnp.float32
    )
    grad_outt = jnp.sum(per_image * image_scale[:, None, None], axis=0)
    summed = lax.psum_scatter(
        jnp.stack([grad_val, grad_outt]).astype(jnp.bfloat16),
        ("dp", "fsdp"),
        scatter_dimension=1,
        tiled=True,
    ).astype(jnp.float32)
    return (summed[0].astype(jnp.bfloat16), summed[1].T.astype(jnp.bfloat16), pair_loss.reshape(1))


def solution(mesh):
    in_specs = (
        P(("dp", "fsdp"), "seq", None, None),
        P(("dp", "fsdp"), "seq", None, None),
        P(("dp", "fsdp"), None),
        P(("dp", "fsdp"), None),
        P(),
        P("fsdp", "seq"),
        P("fsdp", "seq"),
        P("fsdp", "seq"),
        P("seq", "fsdp"),
    )
    out_specs = (P(("dp", "fsdp"), "seq"), P("seq", ("dp", "fsdp")), P(("dp", "fsdp")))
    return jax.shard_map(body, mesh=mesh, in_specs=in_specs, out_specs=out_specs, check_vma=False)
```

profile of v0, /device:TPU:32, one launch (start us, length us, event | category | flops | bytes accessed | tf_op | source)
XLA Modules:
  0.0 666.7 jit_solution(16328834935174783995)
XLA Ops:
  7.2 0.7 broadcast_subtract_fusion
  7.9 0.7 multiply_bitcast_fusion
  8.5 2.7 fusion.13
  11.3 0.7 all-gather.11.cloned.1.call-update
  12.0 0.7 all-gather.13.cloned.1.call-update
  12.7 0.5 all-gather.9.cloned.1.call-update
  13.3 0.5 all-gather.15.cloned.1.call-update
  13.9 43.5 %all-gather.7.cloned.1.call-done = bf16[512,2,3072]{2,0,1:T(8,128)(2,1)} async-done(((bf16[64,2,3072]{2,0,1:T(8,128)(2,1)}), bf16[512,2,3072]{2,0,1:T(8,128)(2,1)}) %all-gather.7.cloned.1.call-update) | async-done | bytes 6291472 | tf_op jit(solution)/shard_map/all_gather | solution.py:36
  57.4 4.2 fusion.1
  61.7 0.3 copy-done
  62.0 2.7 fusion.3
  64.8 29.4 %copy.25 = bf16[512,2,3072]{2,1,0:T(2,128)(2,1)} copy(bf16[512,2,3072]{2,0,1:T(8,128)(2,1)S(1)} %fusion.3) | data formatting | bytes 12582912 | tf_op jit(solution)/shard_map/convert_element_type | solution.py:20
  94.1 13.6 %reshape.83 = bf16[1024,3072]{1,0:T(8,128)(2,1)} reshape(bf16[512,2,3072]{2,1,0:T(2,128)(2,1)} %copy.25) | data formatting | bytes 12582912 | tf_op jit(solution)/shard_map/reshape | solution.py:43
  107.7 34.1 %all-gather.11.cloned.1.call-done = bf16[3072,256]{1,0:T(8,128)(2,1)} async-done(((bf16[192,256]{1,0:T(8,128)(2,1)}), bf16[3072,256]{1,0:T(8,128)(2,1)}) %all-gather.11.cloned.1.call-update) | async-done | bytes 1572880 | tf_op jit(solution)/shard_map/all_gather | solution.py:38
  141.9 5.0 convolution_convert_fusion.3
  146.9 0.1 reshape.85
  147.0 76.4 %all-gather.13.cloned.1.call-done = bf16[3072,256]{1,0:T(8,128)(2,1)} async-done(((bf16[192,256]{1,0:T(8,128)(2,1)}), bf16[3072,256]{1,0:T(8,128)(2,1)}) %all-gather.13.cloned.1.call-update) | async-done | bytes 1572880 | tf_op jit(solution)/shard_map/all_gather | solution.py:39
  223.4 5.0 convolution_convert_fusion.2
  228.4 0.1 reshape.86
  228.5 76.2 %all-gather.9.cloned.1.call-done = bf16[3072,256]{1,0:T(8,128)(2,1)} async-done(((bf16[192,256]{1,0:T(8,128)(2,1)}), bf16[3072,256]{1,0:T(8,128)(2,1)}) %all-gather.9.cloned.1.call-update) | async-done | bytes 1572880 | tf_op jit(solution)/shard_map/all_gather | solution.py:40
  304.7 5.0 convolution_convert_fusion.4
  309.9 0.7 fusion.30
  310.6 2.8 fusion.36
  313.4 0.6 divide_convert_fusion
  314.0 0.5 convolution_convert_fusion.6
  314.5 0.6 copy.30
  315.1 71.0 %all-gather.15.cloned.1.call-done = bf16[256,3072]{0,1:T(8,128)(2,1)} async-done(((bf16[256,192]{0,1:T(8,128)(2,1)}), bf16[256,3072]{0,1:T(8,128)(2,1)}) %all-gather.15.cloned.1.call-update) | async-done | bytes 1572880 | tf_op jit(solution)/shard_map/all_gather | solution.py:42
  386.1 5.9 convolution_convert_fusion
  392.0 42.3 %reduce-scatter.3.cloned.1.call-done = bf16[128,3072]{1,0:T(8,128)(2,1)} async-done(((bf16[1024,3072]{1,0:T(8,128)(2,1)}), bf16[128,3072]{1,0:T(8,128)(2,1)}) %reduce-scatter.3.cloned.1.call-update) | async-done | bytes 786448 | tf_op jit(solution)/shard_map/reduce_scatter | solution.py:61
  434.3 2.9 reshape.87
  437.2 3.1 fusion.15
  440.4 1.4 convert_subtract_fusion
  441.9 2.3 copy.32
  444.2 3.2 sub.46
  447.4 1.7 multiply_reduce_fusion.2
  449.1 0.1 reduce_sum.46
  449.3 0.6 fusion.34
  449.9 14.3 %psum.7 = f32[2]{0:T(128)S(1)} all-reduce(f32[2]{0:T(128)S(1)} %reduce_sum.47), channel_id=1, replica_groups=mesh['dp'=2,'fsdp'=16,'seq'=8] {'seq'}, use_global_device_ids=true, to_apply=%region_6.7 | all-reduce | flops 2 | bytes 16 | tf_op jit(solution)/shard_map/psum | solution.py:70
  464.2 0.6 fusion.35
  467.4 16.4 %all-gather.17.cloned.1.call-done = bf16[512,2,3072]{2,0,1:T(8,128)(2,1)} async-done(((bf16[64,2,3072]{2,0,1:T(8,128)(2,1)}), bf16[512,2,3072]{2,0,1:T(8,128)(2,1)}) %all-gather.17.cloned.1.call-update) | async-done | bytes 6291472 | tf_op jit(solution)/shard_map/all_gather | solution.py:73
  483.9 5.1 fusion.21
  488.9 0.8 fusion.24
  489.8 0.4 copy.34
  490.2 4.7 fusion.4
  494.9 5.5 multiply_reduce_fusion
  500.4 1.9 pad_maximum_fusion
  502.4 154.9 %reduce-scatter.5.cloned.1.call-done = bf16[2,96,256]{2,1,0:T(8,128)(2,1)} async-done(((bf16[2,3072,256]{2,1,0:T(8,128)(2,1)}), bf16[2,96,256]{2,1,0:T(8,128)(2,1)}) %reduce-scatter.5.cloned.1.call-update) | async-done | bytes 98320 | tf_op jit(solution)/shard_map/reduce_scatter | solution.py:104
  657.3 1.5 slice_bitcast_fusion
  (28 shorter events, 0.6 us)
Async XLA Ops:
  7.2 50.2 %all-gather.7.cloned.1.call-start = ((), (), s32[]{:S(2)}) async-start(), calls=%async_computation.2 | async-start | bytes 7077888 | tf_op jit(solution)/shard_map/all_gather | solution.py:36
  11.2 130.6 %all-gather.11.cloned.1.call-start = ((), (), s32[]{:S(2)}) async-start(), calls=%async_computation.4 | async-start | bytes 1671168 | tf_op jit(solution)/shard_map/all_gather | solution.py:38
  12.0 211.4 %all-gather.13.cloned.1.call-start = ((), (), s32[]{:S(2)}) async-start(), calls=%async_computation.5 | async-start | bytes 1671168 | tf_op jit(solution)/shard_map/all_gather | solution.py:39
  12.7 292.0 %all-gather.9.cloned.1.call-start = ((), (), s32[]{:S(2)}) async-start(), calls=%async_computation.3 | async-start | bytes 1671168 | tf_op jit(solution)/shard_map/all_gather | solution.py:40
  13.3 372.8 %all-gather.15.cloned.1.call-start = ((), (), s32[]{:S(2)}) async-start(), calls=%async_computation.6 | async-start | bytes 1671168 | tf_op jit(solution)/shard_map/all_gather | solution.py:42
  13.9 47.8 %copy-start.3 = (f32[3072]{0:T(1024)S(1)}, f32[3072]{0:T(1024)}, u32[]{:S(2)}) copy-start(f32[3072]{0:T(1024)} %param.14) | copy-start | bytes 36868
  13.9 420.4 %reduce-scatter.3.cloned.1.call-start = ((), (), s32[]{:S(2)}) async-start(), calls=%async_computation.7 | async-start | bytes 7077888 | tf_op jit(solution)/shard_map/reduce_scatter | solution.py:61
  57.4 4.6 copy-start
  392.0 45.3 %copy-start.1 = (bf16[1,64,2,3072]{3,2,1,0:T(2,128)(2,1)S(1)}, bf16[1,64,2,3072]{3,2,1,0:T(2,128)(2,1)}, u32[]{:S(2)}) copy-start(bf16[1,64,2,3072]{3,2,1,0:T(2,128)(2,1)} %param.11) | copy-start | bytes 2359300
  392.0 91.9 %all-gather.17.cloned.1.call-start = ((), (), s32[]{:S(2)}) async-start(), calls=%async_computation.8 | async-start | bytes 7077888 | tf_op jit(solution)/shard_map/all_gather | solution.py:73
  440.4 216.9 %reduce-scatter.5.cloned.1.call-start = ((), (), s32[]{:S(2)}) async-start(), calls=%async_computation.9 | async-start | bytes 3244032 | tf_op jit(solution)/shard_map/reduce_scatter | solution.py:104
  441.9 5.5 copy-start.2
  444.2 5.0 copy-start.4
  444.2 23.2 %copy-start.5 = (f32[2]{0:T(128)S(1)}, f32[2]{0:T(128)}, u32[]{:S(2)}) copy-start(f32[2]{0:T(128)} %constant.37.clone) | copy-start | bytes 28
Sparse Core Ops, SparseCore 0:
  11.3 46.0 all-gather.6
  60.0 81.8 all-gather.10
  144.5 78.8 all-gather.12
  225.8 78.8 all-gather.8
  307.2 78.8 all-gather.14
  392.1 42.1 reduce-scatter.2
  440.5 43.3 all-gather.16
  502.4 154.8 reduce-scatter.4
where the time goes:
time: 669 us; the launch traced here: 667 us
  waiting for transfers between devices  517 us (77%)
  local copies, waits for them, and re-layouts  56 us (8%)
  matrix products  38.1 us (6%)
  other arithmetic  22.5 us (3%)
  between operations  18.2 us (3%)
  blocking collectives  14.3 us (2%)
    reduce_scatter x1, waiting for transfers between devices, body(): lax.psum_scatter(jnp.stack([grad_val, grad_outt]).astype(jnp.bfloat16), (...  155 us
    all_gather x1, waiting for transfers between devices, body(): lax.all_gather(w_key, 'fsdp', axis=0, tiled=True)  76.4 us
    all_gather x1, waiting for transfers between devices, body(): lax.all_gather(w_value, 'fsdp', axis=0, tiled=True)  76.2 us
    all_gather x1, waiting for transfers between devices, body(): out_w = lax.all_gather(w_out, 'fsdp', axis=1, tiled=True)  71 us
    all_gather x1, waiting for transfers between devices, body(): lax.all_gather(noised, 'seq', axis=0, tiled=True)  43.5 us
    reduce_scatter x1, waiting for transfers between devices, body(): lax.psum_scatter(jnp.dot(flat_attended, out_w, preferred_element_type=jnp...  42.3 us
    all_gather x1, waiting for transfers between devices, body(): lax.all_gather(w_query, 'fsdp', axis=0, tiled=True)  34.1 us
    convert_element_type x1, local copies, waits for them, and re-layouts, rms_normed(): return (values * inverse * norm_gain).astype(jnp.bfloat16)  29.4 us
  transfers between devices with their start and end apart: 8, of which 8 were waited for; matrix products, arithmetic and copies ran while one was open for 12% of the time, Pallas kernels for 0%

commit v1 on v0

v1 whole, which is shorter than its diff:
```python
import math

import jax
import jax.numpy as jnp
from jax import lax
from jax.sharding import Mesh, PartitionSpec as P

HD = 128
NSTEP = 1000
LOSS_SCALE = 24576
NZ = 8

preference_beta = 2.0
norm_epsilon = 1e-06

SEQ = ("x", "core")
GROUP = ("dp", "z", "yh")
Y = ("dp", "yh")
bf16 = jnp.bfloat16
f32 = jnp.float32


def shift(value, axis, step, count):
    return lax.ppermute(value, axis, [(i, (i + step) % count) for i in range(count)])


def flip(value, axis, mask, count):
    return lax.ppermute(value, axis, [(i, i ^ mask) for i in range(count)])


def gather_weight(mine, other, y_hi):
    crossed = flip(other, Y, 3, 4)
    first = jnp.where(y_hi == 0, jnp.stack([mine, crossed]), jnp.stack([crossed, mine]))

    def hand_over(blocks):
        low = flip(jnp.stack([block[0] for block in blocks]), Y, 2, 4)
        high = flip(jnp.stack([block[1] for block in blocks]), Y, 3, 4)
        return [(low[i], high[i]) for i in range(len(blocks))]

    held = {0: first}
    given = {}
    right = left = first
    for step in range(1, 4):
        right = shift(right, "z", 1, NZ)
        left = shift(left, "z", NZ - 1, NZ)
        held[NZ - step] = right
        held[step] = left
        keys = [0, NZ - 1, 1] if step == 1 else [NZ - step, step]
        for key, value in zip(keys, hand_over([held[k] for k in keys])):
            given[key] = value
    far_low = shift(right[0], "z", 1, NZ)
    far_high = shift(left[1], "z", NZ - 1, NZ)
    held[4] = (far_low, far_high)
    given[4] = (flip(far_low, Y, 2, 4), flip(far_high, Y, 3, 4))
    own = jnp.concatenate([part for k in range(NZ) for part in (held[k][0], held[k][1])], axis=0)
    rest = jnp.concatenate([part for k in range(NZ) for part in given[k]], axis=0)
    return own, rest


def reduce_gradient(grad, dp, z, y_hi):
    pieces = grad.astype(bf16).reshape(2, NZ, 2, -1, grad.shape[1])
    total = None
    for mask in range(4):
        piece = lax.dynamic_index_in_dim(pieces, dp ^ (mask >> 1), 0, keepdims=False)
        piece = lax.dynamic_index_in_dim(piece, y_hi ^ (mask & 1), 1, keepdims=False)
        term = (piece if mask == 0 else flip(piece, Y, mask, 4)).astype(f32)
        total = term if total is None else total + term
    shares = total.astype(bf16)
    result = None
    for step in range(NZ):
        piece = lax.dynamic_index_in_dim(shares, (z + step) % NZ, 0, keepdims=False)
        term = (piece if step == 0 else shift(piece, "z", step, NZ)).astype(f32)
        result = term if result is None else result + term
    return result.astype(bf16)


def body(latents, noise, timesteps, ref_errors, norm_gain, w_query, w_key, w_value, w_out):
    dp, z, y_hi = lax.axis_index("dp"), lax.axis_index("z"), lax.axis_index("yh")
    local_len, model_width = latents.shape[1], latents.shape[3]
    full_len = local_len * 8
    rows_count = 2 * full_len
    z_rows = model_width // NZ

    def rolled(value, offset, axis):
        twice = jnp.concatenate([value, value], axis=axis)
        return lax.dynamic_slice_in_dim(twice, offset * z_rows, model_width, axis)

    def head(weight, which):
        return jnp.where(which == 0, weight[:, :HD], weight[:, HD:])

    def heads(which):
        return jnp.concatenate([head(w, which) for w in (w_query, w_key, w_value)], axis=1)

    w_out_t = w_out.T
    qkv_w = gather_weight(heads(dp), heads(1 - dp), y_hi)
    out_w = gather_weight(head(w_out_t, dp), head(w_out_t, 1 - dp), y_hi)
    out_w = jnp.concatenate(out_w, axis=1)

    clean32 = rolled(latents[0], z, 2).transpose(1, 0, 2).astype(f32)
    noise32 = rolled(noise[0], z, 2).transpose(1, 0, 2).astype(f32)
    gain = rolled(norm_gain, z, 0)
    sigma = (timesteps[0].astype(f32) + 0.5) / NSTEP
    mixing = sigma[:, None, None]
    noised = ((1.0 - mixing) * clean32 + mixing * noise32).astype(bf16).astype(f32)
    target = noise32 - clean32
    inverse = lax.rsqrt(jnp.mean(noised * noised, axis=-1, keepdims=True) + norm_epsilon)
    normed = (noised * inverse * gain).astype(bf16)
    normed = lax.all_gather(normed, SEQ, axis=1, tiled=True)
    rows = normed.reshape(rows_count, model_width)

    attended, probs = [], []
    for weight in qkv_w:
        qkv = jnp.dot(rows, weight, preferred_element_type=f32).astype(bf16)
        qkv = qkv.reshape(2, full_len, 3 * HD)
        query, keys, values = qkv[..., :HD], qkv[..., HD : 2 * HD], qkv[..., 2 * HD :]
        scores = jnp.einsum("ith,ish->its", query, keys, preferred_element_type=f32) / math.sqrt(HD)
        prob = jax.nn.softmax(scores, axis=-1).astype(bf16)
        probs.append(prob)
        attended.append(
            jnp.einsum("its,ish->ith", prob, values, preferred_element_type=f32).astype(bf16)
        )
    attended = jnp.concatenate(attended, axis=2)
    partial = lax.dot_general(
        attended.reshape(rows_count, 2 * HD),
        out_w,
        (((1,), (1,)), ((), ())),
        preferred_element_type=f32,
    ).astype(bf16)
    predicted = lax.psum_scatter(
        partial.reshape(2, full_len, model_width), SEQ, scatter_dimension=1, tiled=True
    ).astype(f32)
    differ = predicted - target
    residual = lax.all_gather(differ.astype(bf16), SEQ, axis=1, tiled=True)
    sums = jnp.sum(differ * differ, axis=(1, 2))
    sums = sums + flip(sums, "core", 1, 2)
    sums = sums + flip(sums, "x", 1, 4)
    sums = sums + flip(sums, "x", 2, 4)
    errors = sums / (full_len * model_width)
    reference_pair = ref_errors[0]
    margin = errors[0] - reference_pair[0] - (errors[1] - reference_pair[1])
    pair_loss = jax.nn.softplus(preference_beta * margin)
    weight_pair = (
        preference_beta
        * jax.nn.sigmoid(preference_beta * margin)
        * 2.0
        * LOSS_SCALE
        / (full_len * model_width)
    )
    image_scale = jnp.array([1.0, -1.0], f32) * weight_pair

    def placed(grad):
        grad = rolled(grad, (NZ - z) % NZ, 0)
        return jnp.where(dp == 0, grad, jnp.concatenate([grad[:, HD:], grad[:, :HD]], axis=1))

    per_image = lax.dot_general(
        residual, attended, (((1,), (1,)), ((0,), (0,))), preferred_element_type=f32
    )
    grad_out = jnp.sum(per_image * image_scale[:, None, None], axis=0)
    grad_out = reduce_gradient(placed(grad_out.astype(bf16)), dp, z, y_hi)
    d_attended = jnp.dot(
        residual.reshape(rows_count, model_width), out_w, preferred_element_type=f32
    )
    d_attended = d_attended.reshape(2, full_len, 2 * HD) * image_scale[:, None, None]
    d_attended = d_attended.astype(bf16)
    d_values = jnp.concatenate(
        [
            jnp.einsum(
                "its,ith->ish", probs[e], d_attended[..., e * HD : (e + 1) * HD],
                preferred_element_type=f32,
            ).astype(bf16)
            for e in range(2)
        ],
        axis=2,
    )
    grad_value = lax.dot_general(
        rows, d_values.reshape(rows_count, 2 * HD), (((0,), (0,)), ((), ())),
        preferred_element_type=f32,
    )
    grad_value = reduce_gradient(placed(grad_value.astype(bf16)), dp, z, y_hi)
    return grad_value, grad_out.T, pair_loss.reshape(1)


def solution(mesh):
    fine = Mesh(mesh.devices.reshape(2, NZ, 2, 4, 2), ("dp", "z", "yh", "x", "core"))
    fsdp = ("z", "yh")
    in_specs = (
        P(GROUP, SEQ, None, None),
        P(GROUP, SEQ, None, None),
        P(GROUP, None),
        P(GROUP, None),
        P(),
        P(fsdp, SEQ),
        P(fsdp, SEQ),
        P(fsdp, SEQ),
        P(SEQ, fsdp),
    )
    out_specs = (P(GROUP, SEQ), P(SEQ, GROUP), P(GROUP))
    return jax.shard_map(body, mesh=fine, in_specs=in_specs, out_specs=out_specs, check_vma=False)
```

time: 669 us -> 351 us (0.52)
  waiting for transfers between devices: 517 us -> 137 us
  starting transfers between devices: 0.32 us -> 107 us
  local copies, waits for them, and re-layouts: 56 us -> 19.7 us
  blocking collectives: 14.3 us -> 0 us
    all_gather x6 -> x2, waiting for transfers between devices: 318 us -> 29.3 us  [the longest x1 29.3 us: body(): residual = lax.all_gather(differ.astype(bf16), SEQ, axis=1, tiled=True)]
    reduce_scatter x2 -> x1, waiting for transfers between devices: 197 us -> 45.4 us  [body(): lax.psum_scatter(partial.reshape(2, full_len, model_width), SEQ, scatter_...]
    ppermute x0 -> x57, starting transfers between devices: none -> 107 us  [the longest x30 62.9 us: shift(): lax.ppermute(value, axis, [(i, (i + step) % count) for i in range(count)])]
    ppermute x0 -> x57, waiting for transfers between devices: none -> 62.4 us  [the longest x30 33.1 us: shift(): lax.ppermute(value, axis, [(i, (i + step) % count) for i in range(count)])]
    convert_element_type x4 -> x0, local copies, waits for them, and re-layouts: 31.9 us -> none  [the longest x1 29.4 us: rms_normed(): return (values * inverse * norm_gain).astype(jnp.bfloat16)]
    reshape x5 -> x0, local copies, waits for them, and re-layouts: 16.9 us -> none  [the longest x1 13.6 us: body(): rows = normed.reshape(full_len * 2, model_width)]
    psum x1 -> x0, blocking collectives: 14.3 us -> none  [body(): totals = lax.psum(local_sums, 'seq')]
    unnamed x12 -> x96, local copies, waits for them, and re-layouts: 0.37 us -> 13.9 us
  transfers between devices with their start and end apart: 8 -> 60, of which waited for: 8 -> 25; matrix products, arithmetic and copies ran while one was open for 12% -> 7% of each run, Pallas kernels for 0% -> 0%
where the time goes in v1:
time: 351 us; the launch traced here: 345 us
  waiting for transfers between devices  137 us (39%)
  starting transfers between devices  107 us (30%)
  matrix products  36.5 us (10%)
  other arithmetic  25.6 us (7%)
  local copies, waits for them, and re-layouts  19.7 us (6%)
  between operations  18.9 us (5%)
    ppermute x30, starting transfers between devices, shift(): lax.ppermute(value, axis, [(i, (i + step) % count) for i in range(count)])  62.9 us
    reduce_scatter x1, waiting for transfers between devices, body(): lax.psum_scatter(partial.reshape(2, full_len, model_width), SEQ, scatter_...  45.4 us
    ppermute x27, starting transfers between devices, flip(): return lax.ppermute(value, axis, [(i, i ^ mask) for i in range(count)])  43.8 us
    ppermute x30, waiting for transfers between devices, shift(): lax.ppermute(value, axis, [(i, (i + step) % count) for i in range(count)])  33.1 us
    all_gather x1, waiting for transfers between devices, body(): residual = lax.all_gather(differ.astype(bf16), SEQ, axis=1, tiled=True)  29.3 us
    ppermute x27, waiting for transfers between devices, flip(): return lax.ppermute(value, axis, [(i, i ^ mask) for i in range(count)])  29.3 us
    unnamed x96, local copies, waits for them, and re-layouts  13.9 us
    dot_general x2, matrix products, body(): qkv = jnp.dot(rows, weight, preferred_element_type=f32).astype(bf16)  13.9 us
  transfers between devices with their start and end apart: 60, of which 25 were waited for; matrix products, arithmetic and copies ran while one was open for 7% of the time, Pallas kernels for 0%

profile of v1, /device:TPU:32, one launch (start us, length us, event | category | flops | bytes accessed | tf_op | source)
XLA Modules:
  0.0 344.7 jit_solution(3924580980429272502)
XLA Ops:
  9.8 3.1 collective-permute-start
  15.7 2.1 fusion.13
  19.6 5.0 %collective-permute-done.17 = bf16[192,128]{1,0:T(8,128)(2,1)S(1)} collective-permute-done((bf16[192,128]{1,0:T(8,128)(2,1)S(1)}, bf16[192,128]{1,0:T(8,128)(2,1)S(1)}, u32[]{:S(2)}, u32[]{:S(2)}) %collective-permute-start.17) | collective-permute-done | bytes 49184 | tf_op jit(solution)/shard_map/ppermute | solution.py:28
  26.8 4.1 %collective-permute-start.1 = (bf16[2,192,384]{2,1,0:T(8,128)(2,1)S(1)}, bf16[2,192,384]{2,1,0:T(8,128)(2,1)S(1)}, u32[]{:S(2)}, u32[]{:S(2)}) collective-permute-start(bf16[2,192,384]{2,1,0:T(8,128)(2,1)S(1)} %maximum_select_fusion.2), channel_id=1, source_target_pairs={{0,112},{16,0},{32,16},{48,32},{64,48},{80,64},{96,80},{112,96},{1... | collective-permute-start | bytes 884744 | tf_op jit(solution)/shard_map/ppermute | solution.py:24
  32.8 3.0 collective-permute-start.22
  35.9 3.9 %collective-permute-done.22 = bf16[2,192,128]{2,1,0:T(8,128)(2,1)S(1)} collective-permute-done((bf16[2,192,128]{2,1,0:T(8,128)(2,1)S(1)}, bf16[2,192,128]{2,1,0:T(8,128)(2,1)S(1)}, u32[]{:S(2)}, u32[]{:S(2)}) %collective-permute-start.22) | collective-permute-done | bytes 98336 | tf_op jit(solution)/shard_map/ppermute | solution.py:24
  39.8 2.9 collective-permute-start.19
  42.7 2.2 collective-permute-done.19
  46.1 3.0 collective-permute-start.29
  50.1 3.7 %collective-permute-done.20 = bf16[2,192,128]{2,1,0:T(8,128)(2,1)S(1)} collective-permute-done((bf16[2,192,128]{2,1,0:T(8,128)(2,1)S(1)}, bf16[2,192,128]{2,1,0:T(8,128)(2,1)S(1)}, u32[]{:S(2)}, u32[]{:S(2)}) %collective-permute-start.20) | collective-permute-done | bytes 98336 | tf_op jit(solution)/shard_map/ppermute | solution.py:24
  53.8 3.1 collective-permute-start.23
  56.9 2.2 collective-permute-done.23
  60.8 2.9 collective-permute-start.24
  65.5 3.2 collective-permute-start.25
  68.7 2.1 collective-permute-done.25
  72.0 2.7 collective-permute-start.33
  76.2 2.6 collective-permute-start.2
  79.1 9.5 %collective-permute-done.5 = bf16[2,192,384]{2,1,0:T(8,128)(2,1)S(1)} collective-permute-done((bf16[2,192,384]{2,1,0:T(8,128)(2,1)S(1)}, bf16[2,192,384]{2,1,0:T(8,128)(2,1)S(1)}, u32[]{:S(2)}, u32[]{:S(2)}) %collective-permute-start.5) | collective-permute-done | bytes 294944 | tf_op jit(solution)/shard_map/ppermute | solution.py:24
  90.0 2.2 collective-permute-start.12
  97.0 3.5 %collective-permute-done.6 = bf16[2,192,384]{2,1,0:T(8,128)(2,1)S(1)} collective-permute-done((bf16[2,192,384]{2,1,0:T(8,128)(2,1)S(1)}, bf16[2,192,384]{2,1,0:T(8,128)(2,1)S(1)}, u32[]{:S(2)}, u32[]{:S(2)}) %collective-permute-start.6) | collective-permute-done | bytes 294944 | tf_op jit(solution)/shard_map/ppermute | solution.py:24
  103.5 10.3 %collective-permute-start.14 = (bf16[2,192,384]{2,1,0:T(8,128)(2,1)S(1)}, bf16[2,192,384]{2,1,0:T(8,128)(2,1)S(1)}, u32[]{:S(2)}, u32[]{:S(2)}) collective-permute-start(bf16[2,192,384]{2,1,0:T(8,128)(2,1)S(1)} %pad_maximum_fusion.9), channel_id=1, source_target_pairs={{0,136},{8,128},{128,8},{136,0},{1,137},{9,129},{129,9},{137,1},{2... | collective-permute-start | bytes 884744 | tf_op jit(solution)/shard_map/ppermute | solution.py:28
  127.4 6.9 %convolution_convert_fusion.2 = bf16[1024,384]{1,0:T(8,128)(2,1)S(1)} fusion(bf16[1024,3072]{1,0:T(8,128)(2,1)} %bitcast.314, bf16[3072,384]{1,0:T(8,128)(2,1)} %copy-done.11), kind=kOutput, calls=%fused_computation.43 | convolution fusion | flops 2416312320 | bytes 9437184 | tf_op jit(solution)/shard_map/dot_general | solution.py:113
  134.2 2.2 fusion.127
  138.7 7.0 %convolution_convert_fusion.1 = bf16[1024,384]{1,0:T(8,128)(2,1)S(1)} fusion(bf16[1024,3072]{1,0:T(8,128)(2,1)} %bitcast.315, bf16[3072,384]{1,0:T(8,128)(2,1)} %fusion.62), kind=kOutput, calls=%fused_computation.42 | convolution fusion | flops 2416312320 | bytes 9437184 | tf_op jit(solution)/shard_map/dot_general | solution.py:113
  145.7 2.2 fusion.122
  153.9 5.9 %convolution_convert_fusion = bf16[1024,3072]{1,0:T(8,128)(2,1)} fusion(bf16[1024,256]{1,0:T(8,128)(2,1)S(1)} %bitcast.306, bf16[3072,128]{1,0:T(8,128)(2,1)} %copy-done.4, bf16[3072,128]{1,0:T(8,128)(2,1)} %copy-done.5), kind=kOutput, calls=%fused_computation.3 | convolution fusion | flops 1616904192 | bytes 8388608 | tf_op jit(solution)/shard_map/dot_general | solution.py:123
  159.9 45.4 %reduce-scatter.2.cloned.1.call-done = bf16[2,64,3072]{2,1,0:T(8,128)(2,1)} async-done(((bf16[2,512,3072]{2,1,0:T(8,128)(2,1)}), bf16[2,64,3072]{2,1,0:T(8,128)(2,1)}) %reduce-scatter.2.cloned.1.call-update) | async-done | bytes 786448 | tf_op jit(solution)/shard_map/reduce_scatter | solution.py:129
  205.2 2.7 multiply_reduce_fusion.3
  209.9 3.4 collective-permute-done.35
  215.1 3.7 %collective-permute-done.36 = f32[2]{0:T(128)S(1)} collective-permute-done((f32[2]{0:T(128)S(1)}, f32[2]{0:T(128)S(1)}, u32[]{:S(2)}, u32[]{:S(2)}) %collective-permute-start.36) | collective-permute-done | bytes 40 | tf_op jit(solution)/shard_map/ppermute | solution.py:28
  222.0 29.3 %all-gather.5.cloned.1.call-done = bf16[2,512,3072]{2,1,0:T(8,128)(2,1)} async-done(((bf16[2,64,3072]{2,1,0:T(8,128)(2,1)}), bf16[2,512,3072]{2,1,0:T(8,128)(2,1)}) %all-gather.5.cloned.1.call-update) | async-done | bytes 6291472 | tf_op jit(solution)/shard_map/all_gather | solution.py:133
  251.4 5.1 %fusion.19 = bf16[2,512,256]{2,1,0:T(8,128)(2,1)S(1)} fusion(bf16[2,512,3072]{2,1,0:T(8,128)(2,1)} %all-gather.5.cloned.1.call-done, bf16[3072,128]{1,0:T(8,128)(2,1)} %copy-done.4, bf16[3072,128]{1,0:T(8,128)(2,1)} %copy-done.5, f32[2]{0:T(128)S(1)} %broadcast_multiply_fusion), kind=kOutput, calls=%fused_computation.45 | convolution fusion | flops 1614282752 | bytes 8388616 | tf_op jit(solution)/shard_map/dot_general | solution.py:160
  257.5 2.6 multiply_reduce_fusion
  260.2 2.0 fusion.2
  262.2 5.0 %fusion.9 = (bf16[3072,256]{1,0:T(8,128)(2,1)S(1)}, bf16[3072,256]{1,0:T(8,128)(2,1)S(1)}) fusion(s32[]{:T(128)S(6)} %select_n.220, bf16[3072,256]{1,0:T(8,128)(2,1)S(1)} %multiply_reduce_fusion, bf16[3072,256]{1,0:T(8,128)(2,1)S(1)} %fusion.2), kind=kLoop, calls=%fused_computation.25 | loop fusion | flops 6291456 | bytes 6291460 | tf_op jit(solution)/shard_map/concatenate | solution.py:85
  269.0 3.0 collective-permute-start.47
  274.9 2.9 collective-permute-start.37
  278.5 4.2 %collective-permute-done.47 = bf16[8,96,256]{2,1,0:T(8,128)(2,1)} collective-permute-done((bf16[8,96,256]{2,1,0:T(8,128)(2,1)S(1)}, bf16[8,96,256]{2,1,0:T(8,128)(2,1)}, u32[]{:S(2)}, u32[]{:S(2)}) %collective-permute-start.47) | collective-permute-done | bytes 393248 | tf_op jit(solution)/shard_map/ppermute | solution.py:28
  282.6 2.7 collective-permute-start.39
  285.4 5.6 %collective-permute-done.48 = bf16[8,96,256]{2,1,0:T(8,128)(2,1)S(1)} collective-permute-done((bf16[8,96,256]{2,1,0:T(8,128)(2,1)}, bf16[8,96,256]{2,1,0:T(8,128)(2,1)S(1)}, u32[]{:S(2)}, u32[]{:S(2)}) %collective-permute-start.48) | collective-permute-done | bytes 393248 | tf_op jit(solution)/shard_map/ppermute | solution.py:28
  294.9 3.8 %collective-permute-start.51 = (bf16[96,256]{1,0:T(8,128)(2,1)S(1)}, bf16[96,256]{1,0:T(8,128)(2,1)S(1)}, u32[]{:S(2)}, u32[]{:S(2)}) collective-permute-start(bf16[96,256]{1,0:T(8,128)(2,1)S(1)} %get-tuple-element.25), channel_id=1, source_target_pairs={{0,32},{16,48},{32,64},{48,80},{64,96},{80,112},{96,0},{112,16},{1... | collective-permute-start | bytes 147464 | tf_op jit(solution)/shard_map/ppermute | solution.py:24
  299.5 4.7 %collective-permute-start.52 = (bf16[96,256]{1,0:T(8,128)(2,1)S(1)}, bf16[96,256]{1,0:T(8,128)(2,1)S(1)}, u32[]{:S(2)}, u32[]{:S(2)}) collective-permute-start(bf16[96,256]{1,0:T(8,128)(2,1)S(1)} %get-tuple-element.24), channel_id=1, source_target_pairs={{0,48},{16,64},{32,80},{48,96},{64,112},{80,0},{96,16},{112,32},{1... | collective-permute-start | bytes 147464 | tf_op jit(solution)/shard_map/ppermute | solution.py:24
  304.3 3.1 collective-permute-done.38
  307.4 4.8 %collective-permute-start.53 = (bf16[96,256]{1,0:T(8,128)(2,1)S(1)}, bf16[96,256]{1,0:T(8,128)(2,1)S(1)}, u32[]{:S(2)}, u32[]{:S(2)}) collective-permute-start(bf16[96,256]{1,0:T(8,128)(2,1)S(1)} %get-tuple-element.23), channel_id=1, source_target_pairs={{0,64},{16,80},{32,96},{48,112},{64,0},{80,16},{96,32},{112,48},{1... | collective-permute-start | bytes 147464 | tf_op jit(solution)/shard_map/ppermute | solution.py:24
  315.4 3.3 collective-permute-start.56
  318.7 2.5 collective-permute-start.41
  321.8 2.3 collective-permute-start.42
  325.8 4.7 %collective-permute-start.44 = (bf16[96,256]{1,0:T(8,128)(2,1)S(1)}, bf16[96,256]{1,0:T(8,128)(2,1)S(1)}, u32[]{:S(2)}, u32[]{:S(2)}) collective-permute-start(bf16[96,256]{1,0:T(8,128)(2,1)S(1)} %get-tuple-element.29), channel_id=1, source_target_pairs={{0,80},{16,96},{32,112},{48,0},{64,16},{80,32},{96,48},{112,64},{1... | collective-permute-start | bytes 147464 | tf_op jit(solution)/shard_map/ppermute | solution.py:24
  (252 shorter events, 77.3 us)
Async XLA Ops:
  7.2 120.2 %all-gather.3.cloned.1.call-start = ((), (), s32[]{:S(2)}) async-start(), calls=%async_computation.1 | async-start | bytes 7077888 | tf_op jit(solution)/shard_map/all_gather | solution.py:108
  9.8 16.9 %collective-permute-start = (bf16[192,384]{1,0:T(8,128)(2,1)S(1)}, bf16[192,384]{1,0:T(8,128)(2,1)S(1)}, u32[]{:S(2)}, u32[]{:S(2)}) collective-permute-start(bf16[192,384]{1,0:T(8,128)(2,1)S(1)} %pad_maximum_fusion.10), channel_id=1, source_target_pairs={{0,136},{8,128},{128,8},{136,0},{1,137},{9,129},{129,9},{137,1},{2... | collective-permute-start | bytes 442376 | tf_op jit(solution)/shard_map/ppermute | solution.py:28
  19.1 186.1 %reduce-scatter.2.cloned.1.call-start = ((), (), s32[]{:S(2)}) async-start(), calls=%async_computation.2 | async-start | bytes 7077888 | tf_op jit(solution)/shard_map/reduce_scatter | solution.py:129
  24.6 6.4 %collective-permute-start.21 = (bf16[2,192,128]{2,1,0:T(8,128)(2,1)S(1)}, bf16[2,192,128]{2,1,0:T(8,128)(2,1)S(1)}, u32[]{:S(2)}, u32[]{:S(2)}) collective-permute-start(bf16[2,192,128]{2,1,0:T(8,128)(2,1)S(1)} %maximum_select_fusion.3), channel_id=1, source_target_pairs={{0,16},{16,32},{32,48},{48,64},{64,80},{80,96},{96,112},{112,0},{1... | collective-permute-start | bytes 294920 | tf_op jit(solution)/shard_map/ppermute | solution.py:24
  26.8 47.9 %collective-permute-start.1 = (bf16[2,192,384]{2,1,0:T(8,128)(2,1)S(1)}, bf16[2,192,384]{2,1,0:T(8,128)(2,1)S(1)}, u32[]{:S(2)}, u32[]{:S(2)}) collective-permute-start(bf16[2,192,384]{2,1,0:T(8,128)(2,1)S(1)} %maximum_select_fusion.2), channel_id=1, source_target_pairs={{0,112},{16,0},{32,16},{48,32},{64,48},{80,64},{96,80},{112,96},{1... | collective-permute-start | bytes 884744 | tf_op jit(solution)/shard_map/ppermute | solution.py:24
  31.0 41.1 %collective-permute-start.4 = (bf16[2,192,384]{2,1,0:T(8,128)(2,1)S(1)}, bf16[2,192,384]{2,1,0:T(8,128)(2,1)S(1)}, u32[]{:S(2)}, u32[]{:S(2)}) collective-permute-start(bf16[2,192,384]{2,1,0:T(8,128)(2,1)S(1)} %maximum_select_fusion.2), channel_id=1, source_target_pairs={{0,16},{16,32},{32,48},{48,64},{64,80},{80,96},{96,112},{112,0},{1... | collective-permute-start | bytes 884744 | tf_op jit(solution)/shard_map/ppermute | solution.py:24
  32.4 13.7 %collective-permute-start.26 = (bf16[3,192,128]{2,1,0:T(8,128)(2,1)S(1)}, bf16[3,192,128]{2,1,0:T(8,128)(2,1)S(1)}, u32[]{:S(2)}, u32[]{:S(2)}) collective-permute-start(bf16[3,192,128]{2,1,0:T(8,128)(2,1)S(1)} %pad_maximum_fusion.11), channel_id=1, source_target_pairs={{0,128},{8,136},{128,0},{136,8},{1,129},{9,137},{129,1},{137,9},{2... | collective-permute-start | bytes 442376 | tf_op jit(solution)/shard_map/ppermute | solution.py:28
  32.5 16.6 %collective-permute-start.27 = (bf16[3,192,128]{2,1,0:T(8,128)(2,1)S(1)}, bf16[3,192,128]{2,1,0:T(8,128)(2,1)S(1)}, u32[]{:S(2)}, u32[]{:S(2)}) collective-permute-start(bf16[3,192,128]{2,1,0:T(8,128)(2,1)S(1)} %pad_maximum_fusion.12), channel_id=1, source_target_pairs={{0,136},{8,128},{128,8},{136,0},{1,137},{9,129},{129,9},{137,1},{2... | collective-permute-start | bytes 442376 | tf_op jit(solution)/shard_map/ppermute | solution.py:28
  32.8 7.0 %collective-permute-start.22 = (bf16[2,192,128]{2,1,0:T(8,128)(2,1)S(1)}, bf16[2,192,128]{2,1,0:T(8,128)(2,1)S(1)}, u32[]{:S(2)}, u32[]{:S(2)}) collective-permute-start(bf16[2,192,128]{2,1,0:T(8,128)(2,1)S(1)} %collective-permute-done.21), channel_id=1, source_target_pairs={{0,16},{16,32},{32,48},{48,64},{64,80},{80,96},{96,112},{112,0},{1... | collective-permute-start | bytes 294920 | tf_op jit(solution)/shard_map/ppermute | solution.py:24
  44.9 14.6 %collective-permute-start.28 = (bf16[2,192,128]{2,1,0:T(8,128)(2,1)S(1)}, bf16[2,192,128]{2,1,0:T(8,128)(2,1)S(1)}, u32[]{:S(2)}, u32[]{:S(2)}) collective-permute-start(bf16[2,192,128]{2,1,0:T(8,128)(2,1)S(1)} %pad_maximum_fusion.13), channel_id=1, source_target_pairs={{0,128},{8,136},{128,0},{136,8},{1,129},{9,137},{129,1},{137,9},{2... | collective-permute-start | bytes 294920 | tf_op jit(solution)/shard_map/ppermute | solution.py:28
  46.1 14.7 %collective-permute-start.29 = (bf16[2,192,128]{2,1,0:T(8,128)(2,1)S(1)}, bf16[2,192,128]{2,1,0:T(8,128)(2,1)S(1)}, u32[]{:S(2)}, u32[]{:S(2)}) collective-permute-start(bf16[2,192,128]{2,1,0:T(8,128)(2,1)S(1)} %pad_maximum_fusion.14), channel_id=1, source_target_pairs={{0,136},{8,128},{128,8},{136,0},{1,137},{9,129},{129,9},{137,1},{2... | collective-permute-start | bytes 294920 | tf_op jit(solution)/shard_map/ppermute | solution.py:28
  59.1 15.9 %collective-permute-start.30 = (bf16[2,192,128]{2,1,0:T(8,128)(2,1)S(1)}, bf16[2,192,128]{2,1,0:T(8,128)(2,1)S(1)}, u32[]{:S(2)}, u32[]{:S(2)}) collective-permute-start(bf16[2,192,128]{2,1,0:T(8,128)(2,1)S(1)} %pad_maximum_fusion.15), channel_id=1, source_target_pairs={{0,128},{8,136},{128,0},{136,8},{1,129},{9,137},{129,1},{137,9},{2... | collective-permute-start | bytes 294920 | tf_op jit(solution)/shard_map/ppermute | solution.py:28
  59.6 16.6 %collective-permute-start.31 = (bf16[2,192,128]{2,1,0:T(8,128)(2,1)S(1)}, bf16[2,192,128]{2,1,0:T(8,128)(2,1)S(1)}, u32[]{:S(2)}, u32[]{:S(2)}) collective-permute-start(bf16[2,192,128]{2,1,0:T(8,128)(2,1)S(1)} %pad_maximum_fusion.16), channel_id=1, source_target_pairs={{0,136},{8,128},{128,8},{136,0},{1,137},{9,129},{129,9},{137,1},{2... | collective-permute-start | bytes 294920 | tf_op jit(solution)/shard_map/ppermute | solution.py:28
  70.9 7.9 %collective-permute-start.32 = (bf16[192,128]{1,0:T(8,128)(2,1)S(1)}, bf16[192,128]{1,0:T(8,128)(2,1)S(1)}, u32[]{:S(2)}, u32[]{:S(2)}) collective-permute-start(bf16[192,128]{1,0:T(8,128)(2,1)S(1)} %collective-permute-done.24), channel_id=1, source_target_pairs={{0,128},{8,136},{128,0},{136,8},{1,129},{9,137},{129,1},{137,9},{2... | collective-permute-start | bytes 147464 | tf_op jit(solution)/shard_map/ppermute | solution.py:28
  72.0 6.8 %collective-permute-start.33 = (bf16[192,128]{1,0:T(8,128)(2,1)S(1)}, bf16[192,128]{1,0:T(8,128)(2,1)S(1)}, u32[]{:S(2)}, u32[]{:S(2)}) collective-permute-start(bf16[192,128]{1,0:T(8,128)(2,1)S(1)} %collective-permute-done.25), channel_id=1, source_target_pairs={{0,136},{8,128},{128,8},{136,0},{1,137},{9,129},{129,9},{137,1},{2... | collective-permute-start | bytes 147464 | tf_op jit(solution)/shard_map/ppermute | solution.py:28
  74.9 18.8 %collective-permute-start.9 = (bf16[3,192,384]{2,1,0:T(8,128)(2,1)S(1)}, bf16[3,192,384]{2,1,0:T(8,128)(2,1)S(1)}, u32[]{:S(2)}, u32[]{:S(2)}) collective-permute-start(bf16[3,192,384]{2,1,0:T(8,128)(2,1)S(1)} %pad_maximum_fusion.4), channel_id=1, source_target_pairs={{0,128},{8,136},{128,0},{136,8},{1,129},{9,137},{129,1},{137,9},{2... | collective-permute-start | bytes 1327112 | tf_op jit(solution)/shard_map/ppermute | solution.py:28
  75.1 19.9 %collective-permute-start.10 = (bf16[3,192,384]{2,1,0:T(8,128)(2,1)S(1)}, bf16[3,192,384]{2,1,0:T(8,128)(2,1)S(1)}, u32[]{:S(2)}, u32[]{:S(2)}) collective-permute-start(bf16[3,192,384]{2,1,0:T(8,128)(2,1)S(1)} %pad_maximum_fusion.5), channel_id=1, source_target_pairs={{0,136},{8,128},{128,8},{136,0},{1,137},{9,129},{129,9},{137,1},{2... | collective-permute-start | bytes 1327112 | tf_op jit(solution)/shard_map/ppermute | solution.py:28
  76.2 12.4 %collective-permute-start.2 = (bf16[2,192,384]{2,1,0:T(8,128)(2,1)S(1)}, bf16[2,192,384]{2,1,0:T(8,128)(2,1)S(1)}, u32[]{:S(2)}, u32[]{:S(2)}) collective-permute-start(bf16[2,192,384]{2,1,0:T(8,128)(2,1)S(1)} %collective-permute-done.1), channel_id=1, source_target_pairs={{0,112},{16,0},{32,16},{48,32},{64,48},{80,64},{96,80},{112,96},{1... | collective-permute-start | bytes 884744 | tf_op jit(solution)/shard_map/ppermute | solution.py:24
  78.7 9.8 %collective-permute-start.5 = (bf16[2,192,384]{2,1,0:T(8,128)(2,1)S(1)}, bf16[2,192,384]{2,1,0:T(8,128)(2,1)S(1)}, u32[]{:S(2)}, u32[]{:S(2)}) collective-permute-start(bf16[2,192,384]{2,1,0:T(8,128)(2,1)S(1)} %collective-permute-done.4), channel_id=1, source_target_pairs={{0,16},{16,32},{32,48},{48,64},{64,80},{80,96},{96,112},{112,0},{1... | collective-permute-start | bytes 884744 | tf_op jit(solution)/shard_map/ppermute | solution.py:24
  88.7 14.8 %collective-permute-start.11 = (bf16[2,192,384]{2,1,0:T(8,128)(2,1)S(1)}, bf16[2,192,384]{2,1,0:T(8,128)(2,1)S(1)}, u32[]{:S(2)}, u32[]{:S(2)}) collective-permute-start(bf16[2,192,384]{2,1,0:T(8,128)(2,1)S(1)} %pad_maximum_fusion.6), channel_id=1, source_target_pairs={{0,128},{8,136},{128,0},{136,8},{1,129},{9,137},{129,1},{137,9},{2... | collective-permute-start | bytes 884744 | tf_op jit(solution)/shard_map/ppermute | solution.py:28
  90.0 24.5 %collective-permute-start.12 = (bf16[2,192,384]{2,1,0:T(8,128)(2,1)S(1)}, bf16[2,192,384]{2,1,0:T(8,128)(2,1)S(1)}, u32[]{:S(2)}, u32[]{:S(2)}) collective-permute-start(bf16[2,192,384]{2,1,0:T(8,128)(2,1)S(1)} %pad_maximum_fusion.7), channel_id=1, source_target_pairs={{0,136},{8,128},{128,8},{136,0},{1,137},{9,129},{129,9},{137,1},{2... | collective-permute-start | bytes 884744 | tf_op jit(solution)/shard_map/ppermute | solution.py:28
  92.1 9.0 %collective-permute-start.3 = (bf16[2,192,384]{2,1,0:T(8,128)(2,1)S(1)}, bf16[2,192,384]{2,1,0:T(8,128)(2,1)S(1)}, u32[]{:S(2)}, u32[]{:S(2)}) collective-permute-start(bf16[2,192,384]{2,1,0:T(8,128)(2,1)S(1)} %collective-permute-done.2), channel_id=1, source_target_pairs={{0,112},{16,0},{32,16},{48,32},{64,48},{80,64},{96,80},{112,96},{1... | collective-permute-start | bytes 884744 | tf_op jit(solution)/shard_map/ppermute | solution.py:24
  93.7 6.8 %collective-permute-start.6 = (bf16[2,192,384]{2,1,0:T(8,128)(2,1)S(1)}, bf16[2,192,384]{2,1,0:T(8,128)(2,1)S(1)}, u32[]{:S(2)}, u32[]{:S(2)}) collective-permute-start(bf16[2,192,384]{2,1,0:T(8,128)(2,1)S(1)} %collective-permute-done.5), channel_id=1, source_target_pairs={{0,16},{16,32},{32,48},{48,64},{64,80},{80,96},{96,112},{112,0},{1... | collective-permute-start | bytes 884744 | tf_op jit(solution)/shard_map/ppermute | solution.py:24
  100.5 14.6 %collective-permute-start.7 = (bf16[192,384]{1,0:T(8,128)(2,1)S(1)}, bf16[192,384]{1,0:T(8,128)(2,1)S(1)}, u32[]{:S(2)}, u32[]{:S(2)}) collective-permute-start(bf16[192,384]{1,0:T(8,128)(2,1)S(1)} %get-tuple-element.36), channel_id=1, source_target_pairs={{0,16},{16,32},{32,48},{48,64},{64,80},{80,96},{96,112},{112,0},{1... | collective-permute-start | bytes 442376 | tf_op jit(solution)/shard_map/ppermute | solution.py:24
  101.2 15.1 %collective-permute-start.8 = (bf16[192,384]{1,0:T(8,128)(2,1)S(1)}, bf16[192,384]{1,0:T(8,128)(2,1)S(1)}, u32[]{:S(2)}, u32[]{:S(2)}) collective-permute-start(bf16[192,384]{1,0:T(8,128)(2,1)S(1)} %get-tuple-element.33), channel_id=1, source_target_pairs={{0,112},{16,0},{32,16},{48,32},{64,48},{80,64},{96,80},{112,96},{1... | collective-permute-start | bytes 442376 | tf_op jit(solution)/shard_map/ppermute | solution.py:24
  102.8 15.5 %collective-permute-start.13 = (bf16[2,192,384]{2,1,0:T(8,128)(2,1)S(1)}, bf16[2,192,384]{2,1,0:T(8,128)(2,1)S(1)}, u32[]{:S(2)}, u32[]{:S(2)}) collective-permute-start(bf16[2,192,384]{2,1,0:T(8,128)(2,1)S(1)} %pad_maximum_fusion.8), channel_id=1, source_target_pairs={{0,128},{8,136},{128,0},{136,8},{1,129},{9,137},{129,1},{137,9},{2... | collective-permute-start | bytes 884744 | tf_op jit(solution)/shard_map/ppermute | solution.py:28
  103.5 16.9 %collective-permute-start.14 = (bf16[2,192,384]{2,1,0:T(8,128)(2,1)S(1)}, bf16[2,192,384]{2,1,0:T(8,128)(2,1)S(1)}, u32[]{:S(2)}, u32[]{:S(2)}) collective-permute-start(bf16[2,192,384]{2,1,0:T(8,128)(2,1)S(1)} %pad_maximum_fusion.9), channel_id=1, source_target_pairs={{0,136},{8,128},{128,8},{136,0},{1,137},{9,129},{129,9},{137,1},{2... | collective-permute-start | bytes 884744 | tf_op jit(solution)/shard_map/ppermute | solution.py:28
  115.2 6.0 %collective-permute-start.15 = (bf16[192,384]{1,0:T(8,128)(2,1)S(1)}, bf16[192,384]{1,0:T(8,128)(2,1)S(1)}, u32[]{:S(2)}, u32[]{:S(2)}) collective-permute-start(bf16[192,384]{1,0:T(8,128)(2,1)S(1)} %collective-permute-done.7), channel_id=1, source_target_pairs={{0,128},{8,136},{128,0},{136,8},{1,129},{9,137},{129,1},{137,9},{2... | collective-permute-start | bytes 442376 | tf_op jit(solution)/shard_map/ppermute | solution.py:28
  116.3 6.4 %collective-permute-start.16 = (bf16[192,384]{1,0:T(8,128)(2,1)S(1)}, bf16[192,384]{1,0:T(8,128)(2,1)S(1)}, u32[]{:S(2)}, u32[]{:S(2)}) collective-permute-start(bf16[192,384]{1,0:T(8,128)(2,1)S(1)} %collective-permute-done.8), channel_id=1, source_target_pairs={{0,136},{8,128},{128,8},{136,0},{1,137},{9,129},{129,9},{137,1},{2... | collective-permute-start | bytes 442376 | tf_op jit(solution)/shard_map/ppermute | solution.py:28
  159.8 91.5 %all-gather.5.cloned.1.call-start = ((), (), s32[]{:S(2)}) async-start(), calls=%async_computation.3 | async-start | bytes 7077888 | tf_op jit(solution)/shard_map/all_gather | solution.py:133
  269.0 13.6 %collective-permute-start.47 = (bf16[8,96,256]{2,1,0:T(8,128)(2,1)S(1)}, bf16[8,96,256]{2,1,0:T(8,128)(2,1)}, u32[]{:S(2)}, u32[]{:S(2)}) collective-permute-start(bf16[8,96,256]{2,1,0:T(8,128)(2,1)S(1)} %get-tuple-element.9), channel_id=1, source_target_pairs={{0,8},{8,0},{128,136},{136,128},{1,9},{9,1},{129,137},{137,129},{2... | collective-permute-start | bytes 1179656 | tf_op jit(solution)/shard_map/ppermute | solution.py:28
  272.1 19.0 %collective-permute-start.48 = (bf16[8,96,256]{2,1,0:T(8,128)(2,1)}, bf16[8,96,256]{2,1,0:T(8,128)(2,1)S(1)}, u32[]{:S(2)}, u32[]{:S(2)}) collective-permute-start(bf16[8,96,256]{2,1,0:T(8,128)(2,1)} %get-tuple-element.11), channel_id=1, source_target_pairs={{0,128},{8,136},{128,0},{136,8},{1,129},{9,137},{129,1},{137,9},{2... | collective-permute-start | bytes 1179656 | tf_op jit(solution)/shard_map/ppermute | solution.py:28
  272.6 19.1 %collective-permute-start.49 = (bf16[8,96,256]{2,1,0:T(8,128)(2,1)}, bf16[8,96,256]{2,1,0:T(8,128)(2,1)}, u32[]{:S(2)}, u32[]{:S(2)}) collective-permute-start(bf16[8,96,256]{2,1,0:T(8,128)(2,1)} %get-tuple-element.10), channel_id=1, source_target_pairs={{0,136},{8,128},{128,8},{136,0},{1,137},{9,129},{129,9},{137,1},{2... | collective-permute-start | bytes 1179656 | tf_op jit(solution)/shard_map/ppermute | solution.py:28
  274.9 24.6 %collective-permute-start.37 = (bf16[8,96,256]{2,1,0:T(8,128)(2,1)}, bf16[8,96,256]{2,1,0:T(8,128)(2,1)}, u32[]{:S(2)}, u32[]{:S(2)}) collective-permute-start(bf16[8,96,256]{2,1,0:T(8,128)(2,1)} %get-tuple-element.14), channel_id=1, source_target_pairs={{0,8},{8,0},{128,136},{136,128},{1,9},{9,1},{129,137},{137,129},{2... | collective-permute-start | bytes 1179656 | tf_op jit(solution)/shard_map/ppermute | solution.py:28
  277.9 29.5 %collective-permute-start.38 = (bf16[8,96,256]{2,1,0:T(8,128)(2,1)}, bf16[8,96,256]{2,1,0:T(8,128)(2,1)}, u32[]{:S(2)}, u32[]{:S(2)}) collective-permute-start(bf16[8,96,256]{2,1,0:T(8,128)(2,1)} %get-tuple-element.16), channel_id=1, source_target_pairs={{0,128},{8,136},{128,0},{136,8},{1,129},{9,137},{129,1},{137,9},{2... | collective-permute-start | bytes 1179656 | tf_op jit(solution)/shard_map/ppermute | solution.py:28
  282.6 29.6 %collective-permute-start.39 = (bf16[8,96,256]{2,1,0:T(8,128)(2,1)}, bf16[8,96,256]{2,1,0:T(8,128)(2,1)}, u32[]{:S(2)}, u32[]{:S(2)}) collective-permute-start(bf16[8,96,256]{2,1,0:T(8,128)(2,1)} %get-tuple-element.15), channel_id=1, source_target_pairs={{0,136},{8,128},{128,8},{136,0},{1,137},{9,129},{129,9},{137,1},{2... | collective-permute-start | bytes 1179656 | tf_op jit(solution)/shard_map/ppermute | solution.py:28
  293.3 21.6 %collective-permute-start.50 = (bf16[96,256]{1,0:T(8,128)(2,1)S(1)}, bf16[96,256]{1,0:T(8,128)(2,1)S(1)}, u32[]{:S(2)}, u32[]{:S(2)}) collective-permute-start(bf16[96,256]{1,0:T(8,128)(2,1)S(1)} %get-tuple-element.19), channel_id=1, source_target_pairs={{0,16},{16,32},{32,48},{48,64},{64,80},{80,96},{96,112},{112,0},{1... | collective-permute-start | bytes 147464 | tf_op jit(solution)/shard_map/ppermute | solution.py:24
  294.9 20.5 %collective-permute-start.51 = (bf16[96,256]{1,0:T(8,128)(2,1)S(1)}, bf16[96,256]{1,0:T(8,128)(2,1)S(1)}, u32[]{:S(2)}, u32[]{:S(2)}) collective-permute-start(bf16[96,256]{1,0:T(8,128)(2,1)S(1)} %get-tuple-element.25), channel_id=1, source_target_pairs={{0,32},{16,48},{32,64},{48,80},{64,96},{80,112},{96,0},{112,16},{1... | collective-permute-start | bytes 147464 | tf_op jit(solution)/shard_map/ppermute | solution.py:24
  299.5 19.1 %collective-permute-start.52 = (bf16[96,256]{1,0:T(8,128)(2,1)S(1)}, bf16[96,256]{1,0:T(8,128)(2,1)S(1)}, u32[]{:S(2)}, u32[]{:S(2)}) collective-permute-start(bf16[96,256]{1,0:T(8,128)(2,1)S(1)} %get-tuple-element.24), channel_id=1, source_target_pairs={{0,48},{16,64},{32,80},{48,96},{64,112},{80,0},{96,16},{112,32},{1... | collective-permute-start | bytes 147464 | tf_op jit(solution)/shard_map/ppermute | solution.py:24
  307.4 11.3 %collective-permute-start.53 = (bf16[96,256]{1,0:T(8,128)(2,1)S(1)}, bf16[96,256]{1,0:T(8,128)(2,1)S(1)}, u32[]{:S(2)}, u32[]{:S(2)}) collective-permute-start(bf16[96,256]{1,0:T(8,128)(2,1)S(1)} %get-tuple-element.23), channel_id=1, source_target_pairs={{0,64},{16,80},{32,96},{48,112},{64,0},{80,16},{96,32},{112,48},{1... | collective-permute-start | bytes 147464 | tf_op jit(solution)/shard_map/ppermute | solution.py:24
  312.2 9.6 %collective-permute-start.54 = (bf16[96,256]{1,0:T(8,128)(2,1)S(1)}, bf16[96,256]{1,0:T(8,128)(2,1)S(1)}, u32[]{:S(2)}, u32[]{:S(2)}) collective-permute-start(bf16[96,256]{1,0:T(8,128)(2,1)S(1)} %get-tuple-element.22), channel_id=1, source_target_pairs={{0,80},{16,96},{32,112},{48,0},{64,16},{80,32},{96,48},{112,64},{1... | collective-permute-start | bytes 147464 | tf_op jit(solution)/shard_map/ppermute | solution.py:24
  314.9 9.3 %collective-permute-start.55 = (bf16[96,256]{1,0:T(8,128)(2,1)S(1)}, bf16[96,256]{1,0:T(8,128)(2,1)S(1)}, u32[]{:S(2)}, u32[]{:S(2)}) collective-permute-start(bf16[96,256]{1,0:T(8,128)(2,1)S(1)} %get-tuple-element.21), channel_id=1, source_target_pairs={{0,96},{16,112},{32,0},{48,16},{64,32},{80,48},{96,64},{112,80},{1... | collective-permute-start | bytes 147464 | tf_op jit(solution)/shard_map/ppermute | solution.py:24
  315.4 10.5 %collective-permute-start.56 = (bf16[96,256]{1,0:T(8,128)(2,1)S(1)}, bf16[96,256]{1,0:T(8,128)(2,1)S(1)}, u32[]{:S(2)}, u32[]{:S(2)}) collective-permute-start(bf16[96,256]{1,0:T(8,128)(2,1)S(1)} %get-tuple-element.20), channel_id=1, source_target_pairs={{0,112},{16,0},{32,16},{48,32},{64,48},{80,64},{96,80},{112,96},{1... | collective-permute-start | bytes 147464 | tf_op jit(solution)/shard_map/ppermute | solution.py:24
  318.7 11.9 %collective-permute-start.40 = (bf16[96,256]{1,0:T(8,128)(2,1)S(1)}, bf16[96,256]{1,0:T(8,128)(2,1)S(1)}, u32[]{:S(2)}, u32[]{:S(2)}) collective-permute-start(bf16[96,256]{1,0:T(8,128)(2,1)S(1)} %get-tuple-element.26), channel_id=1, source_target_pairs={{0,16},{16,32},{32,48},{48,64},{64,80},{80,96},{96,112},{112,0},{1... | collective-permute-start | bytes 147464 | tf_op jit(solution)/shard_map/ppermute | solution.py:24
  318.7 12.8 %collective-permute-start.41 = (bf16[96,256]{1,0:T(8,128)(2,1)S(1)}, bf16[96,256]{1,0:T(8,128)(2,1)S(1)}, u32[]{:S(2)}, u32[]{:S(2)}) collective-permute-start(bf16[96,256]{1,0:T(8,128)(2,1)S(1)} %get-tuple-element.32), channel_id=1, source_target_pairs={{0,32},{16,48},{32,64},{48,80},{64,96},{80,112},{96,0},{112,16},{1... | collective-permute-start | bytes 147464 | tf_op jit(solution)/shard_map/ppermute | solution.py:24
  321.8 12.0 %collective-permute-start.42 = (bf16[96,256]{1,0:T(8,128)(2,1)S(1)}, bf16[96,256]{1,0:T(8,128)(2,1)S(1)}, u32[]{:S(2)}, u32[]{:S(2)}) collective-permute-start(bf16[96,256]{1,0:T(8,128)(2,1)S(1)} %get-tuple-element.31), channel_id=1, source_target_pairs={{0,48},{16,64},{32,80},{48,96},{64,112},{80,0},{96,16},{112,32},{1... | collective-permute-start | bytes 147464 | tf_op jit(solution)/shard_map/ppermute | solution.py:24
  324.2 9.7 %collective-permute-start.43 = (bf16[96,256]{1,0:T(8,128)(2,1)S(1)}, bf16[96,256]{1,0:T(8,128)(2,1)S(1)}, u32[]{:S(2)}, u32[]{:S(2)}) collective-permute-start(bf16[96,256]{1,0:T(8,128)(2,1)S(1)} %get-tuple-element.30), channel_id=1, source_target_pairs={{0,64},{16,80},{32,96},{48,112},{64,0},{80,16},{96,32},{112,48},{1... | collective-permute-start | bytes 147464 | tf_op jit(solution)/shard_map/ppermute | solution.py:24
  325.8 8.5 %collective-permute-start.44 = (bf16[96,256]{1,0:T(8,128)(2,1)S(1)}, bf16[96,256]{1,0:T(8,128)(2,1)S(1)}, u32[]{:S(2)}, u32[]{:S(2)}) collective-permute-start(bf16[96,256]{1,0:T(8,128)(2,1)S(1)} %get-tuple-element.29), channel_id=1, source_target_pairs={{0,80},{16,96},{32,112},{48,0},{64,16},{80,32},{96,48},{112,64},{1... | collective-permute-start | bytes 147464 | tf_op jit(solution)/shard_map/ppermute | solution.py:24
  (29 other events, 246.4 us)
Sparse Core Ops, SparseCore 0:
  19.3 43.4 all-gather.2
  159.9 45.2 reduce-scatter.1
  208.1 43.1 all-gather.4

commit v2 on v1

v2 whole, which is shorter than its diff:
```python
import functools
import math

import jax
import jax.numpy as jnp
from jax import lax
from jax.experimental import pallas as pl
from jax.experimental.pallas import tpu as pltpu
from jax.sharding import Mesh, PartitionSpec as P

HD = 128
NSTEP = 1000
LOSS_SCALE = 24576
NZ = 8

preference_beta = 2.0
norm_epsilon = 1e-06

SEQ = ("x", "core")
GROUP = ("dp", "z", "yh")
Y = ("dp", "yh")
bf16 = jnp.bfloat16
f32 = jnp.float32


def shift(value, axis, step, count):
    return lax.ppermute(value, axis, [(i, (i + step) % count) for i in range(count)])


def flip(value, axis, mask, count):
    return lax.ppermute(value, axis, [(i, i ^ mask) for i in range(count)])


def gather_weight(mine, other, y_hi):
    crossed = flip(other, Y, 3, 4)
    first = jnp.where(y_hi == 0, jnp.stack([mine, crossed]), jnp.stack([crossed, mine]))
    own, rest = {0: first}, {}

    def hand_over(keys):
        low = flip(jnp.stack([own[k][0] for k in keys]), Y, 2, 4)
        high = flip(jnp.stack([own[k][1] for k in keys]), Y, 3, 4)
        for i, k in enumerate(keys):
            rest[k] = ((low, i), (high, i))

    right = left = first
    for step in range(1, 4):
        right = shift(right, "z", 1, NZ)
        left = shift(left, "z", NZ - 1, NZ)
        own[NZ - step], own[step] = right, left
        hand_over([0, NZ - 1, 1] if step == 1 else [NZ - step, step])
    far_low = shift(right[0:1], "z", 1, NZ)
    far_high = shift(left[1:2], "z", NZ - 1, NZ)
    far = ((far_low, 0), (far_high, 0))
    rest[4] = ((flip(far_low, Y, 2, 4), 0), (flip(far_high, Y, 3, 4), 0))
    own = [far if k == 4 else ((own[k], 0), (own[k], 1)) for k in range(NZ)]
    return own, [rest[k] for k in range(NZ)]


def forward_kernel(places, count, normed, *refs):
    weights = refs[:count]
    attended, probs, partial, out_w, qkv_w, qkv = refs[count:]
    image, tile = pl.program_id(0), pl.program_id(1)
    tile_rows = normed.shape[1]

    @pl.when((image == 0) & (tile == 0))
    def _():
        for e in range(2):
            for k in range(2 * NZ):
                which, index = places[e][k]
                block = weights[which][index]
                rows = slice(k * 192, k * 192 + 192)
                qkv_w[rows, e * 384 : e * 384 + 384] = block[:, :384]
                out_w[rows, e * HD : e * HD + HD] = block[:, 384:]

    product = jnp.dot(normed[0], qkv_w[...], preferred_element_type=f32)
    start = pl.multiple_of(tile * tile_rows, tile_rows)
    qkv[pl.ds(start, tile_rows), :] = product.astype(bf16)

    @pl.when(tile == pl.num_programs(1) - 1)
    def _():
        for e in range(2):
            base = e * 384
            query, keys = qkv[:, base : base + HD], qkv[:, base + HD : base + 2 * HD]
            scores = lax.dot_general(
                query, keys, (((1,), (1,)), ((), ())), preferred_element_type=f32
            ) * (1.0 / math.sqrt(HD))
            weight = jnp.exp(scores - jnp.max(scores, axis=-1, keepdims=True))
            prob = (weight / jnp.sum(weight, axis=-1, keepdims=True)).astype(bf16)
            probs[0, e] = prob
            attended[0, :, e * HD : e * HD + HD] = jnp.dot(
                prob, qkv[:, base + 2 * HD : base + 384], preferred_element_type=f32
            ).astype(bf16)
        for chunk in range(4):
            part = slice(chunk * 768, chunk * 768 + 768)
            partial[0, :, part] = lax.dot_general(
                attended[0], out_w[part, :], (((1,), (1,)), ((), ())), preferred_element_type=f32
            ).astype(bf16)


def forward(normed, own, rest):
    arrays, places = [], []
    for blocks in (own, rest):
        places.append([])
        for pair in blocks:
            for array, index in pair:
                known = [i for i, a in enumerate(arrays) if a is array]
                if not known:
                    arrays.append(array)
                    known = [len(arrays) - 1]
                places[-1].append((known[0], index))
    _, length, width = normed.shape
    tiles = 2
    shapes = (
        ((2, length, 2 * HD), (1, length, 2 * HD), lambda i, t: (i, 0, 0)),
        ((2, 2, length, length), (1, 2, length, length), lambda i, t: (i, 0, 0, 0)),
        ((2, length, width), (1, length, width), lambda i, t: (i, 0, 0)),
        ((width, 2 * HD), (width, 2 * HD), lambda i, t: (0, 0)),
    )
    return pl.pallas_call(
        functools.partial(forward_kernel, places, len(arrays)),
        grid=(2, tiles),
        in_specs=[pl.BlockSpec((1, length // tiles, width), lambda i, t: (i, t, 0))]
        + [pl.BlockSpec(a.shape, lambda i, t: (0, 0, 0)) for a in arrays],
        out_specs=[pl.BlockSpec(block, index) for _, block, index in shapes],
        out_shape=[jax.ShapeDtypeStruct(shape, bf16) for shape, _, _ in shapes],
        scratch_shapes=[
            pltpu.VMEM((width, 6 * HD), bf16),
            pltpu.VMEM((length, 6 * HD), bf16),
        ],
        compiler_params=pltpu.CompilerParams(vmem_limit_bytes=60 * 2**20),
        name="forward",
    )(normed, *arrays)


def store_placed(grad, position, total):
    z, dp = position[0], position[1]
    for k in range(NZ):
        block = total[:, k * 384 : k * 384 + 384].astype(bf16)
        start = pl.multiple_of(lax.rem(z + k, NZ) * 384, 384)
        for e in range(2):
            column = pl.multiple_of((dp ^ e) * HD, HD)
            grad[pl.ds(start, 384), pl.ds(column, HD)] = block[e * HD : e * HD + HD].T


def grad_out_kernel(position, scale, residual, attended, grad, total):
    image = pl.program_id(0)
    term = jnp.dot(attended[0].T, residual[0], preferred_element_type=f32) * scale[image]

    @pl.when(image == 0)
    def _():
        total[...] = term

    @pl.when(image == 1)
    def _():
        total[...] += term
        store_placed(grad, position, total)


def grad_value_kernel(position, scale, residual, normed, probs, out_w, grad, total):
    image = pl.program_id(0)
    d_attended = jnp.dot(residual[0], out_w[...], preferred_element_type=f32) * scale[image]
    d_attended = d_attended.astype(bf16)
    d_values = jnp.concatenate(
        [
            lax.dot_general(
                d_attended[:, e * HD : e * HD + HD].T, probs[0, e], (((1,), (0,)), ((), ())),
                preferred_element_type=f32,
            ).astype(bf16)
            for e in range(2)
        ],
        axis=0,
    )
    term = jnp.dot(d_values, normed[0], preferred_element_type=f32)

    @pl.when(image == 0)
    def _():
        total[...] = term

    @pl.when(image == 1)
    def _():
        total[...] += term
        store_placed(grad, position, total)


def gradient(kernel, name, position, scale, images, shared):
    width = images[0].shape[2]

    def image_spec(a):
        zeros = (0,) * (a.ndim - 1)
        return pl.BlockSpec((1,) + a.shape[1:], lambda i: (i,) + zeros)

    smem = pl.BlockSpec(memory_space=pltpu.SMEM)
    return pl.pallas_call(
        kernel,
        grid=(2,),
        in_specs=[smem, smem]
        + [image_spec(a) for a in images]
        + [pl.BlockSpec(a.shape, lambda i: (0, 0)) for a in shared],
        out_specs=pl.BlockSpec((width, 2 * HD), lambda i: (0, 0)),
        out_shape=jax.ShapeDtypeStruct((width, 2 * HD), bf16),
        scratch_shapes=[pltpu.VMEM((2 * HD, width), f32)],
        compiler_params=pltpu.CompilerParams(vmem_limit_bytes=60 * 2**20),
        name=name,
    )(position, scale, *images, *shared)


def reduce_y(grad, dp, y_hi):
    pieces = grad.reshape(2, NZ, 2, -1, grad.shape[1])

    def piece(mask, part):
        chosen = lax.dynamic_index_in_dim(pieces, dp ^ (mask >> 1), 0, keepdims=False)
        chosen = lax.dynamic_index_in_dim(chosen, y_hi ^ (mask & 1), 1, keepdims=False)
        return chosen[part]

    sums = []
    for part, near, across in ((slice(0, 4), 2, 3), (slice(4, 8), 3, 2)):
        came = flip(jnp.stack([piece(near, part), piece(1, part)]), Y, near, 4).astype(f32)
        passed = (piece(across, part).astype(f32) + came[1]).astype(bf16)
        sums.append(piece(0, part).astype(f32) + came[0] + flip(passed, Y, across, 4).astype(f32))
    return jnp.concatenate(sums, axis=0).astype(bf16)


def reduce_z(shares, z):
    result = None
    for step in range(NZ):
        piece = lax.dynamic_index_in_dim(shares, (z + step) % NZ, 1, keepdims=False)
        term = (piece if step == 0 else shift(piece, "z", step, NZ)).astype(f32)
        result = term if result is None else result + term
    return result.astype(bf16)


def body(latents, noise, timesteps, ref_errors, norm_gain, w_query, w_key, w_value, w_out):
    dp, z, y_hi = lax.axis_index("dp"), lax.axis_index("z"), lax.axis_index("yh")
    local_len, model_width = latents.shape[1], latents.shape[3]
    full_len = local_len * 8
    z_rows = model_width // NZ

    def rolled(value, offset, axis):
        twice = jnp.concatenate([value, value], axis=axis)
        return lax.dynamic_slice_in_dim(twice, offset * z_rows, model_width, axis)

    def head(weight, which):
        return jnp.where(which == 0, weight[:, :HD], weight[:, HD:])

    def heads(which):
        return jnp.concatenate([head(w, which) for w in (w_query, w_key, w_value, w_out.T)], axis=1)

    own, rest = gather_weight(heads(dp), heads(1 - dp), y_hi)

    clean32 = rolled(latents[0], z, 2).transpose(1, 0, 2).astype(f32)
    noise32 = rolled(noise[0], z, 2).transpose(1, 0, 2).astype(f32)
    gain = rolled(norm_gain, z, 0)
    sigma = (timesteps[0].astype(f32) + 0.5) / NSTEP
    mixing = sigma[:, None, None]
    noised = ((1.0 - mixing) * clean32 + mixing * noise32).astype(bf16).astype(f32)
    target = noise32 - clean32
    inverse = lax.rsqrt(jnp.mean(noised * noised, axis=-1, keepdims=True) + norm_epsilon)
    normed = (noised * inverse * gain).astype(bf16)
    normed = lax.all_gather(normed, SEQ, axis=1, tiled=True)
    attended, probs, partial, out_w = forward(normed, own, rest)
    predicted = lax.psum_scatter(
        partial, SEQ, scatter_dimension=1, tiled=True
    ).astype(f32)
    differ = predicted - target
    residual = lax.all_gather(differ.astype(bf16), SEQ, axis=1, tiled=True)
    sums = jnp.sum(differ * differ, axis=(1, 2))
    sums = sums + flip(sums, "core", 1, 2)
    sums = sums + flip(sums, "x", 1, 4)
    sums = sums + flip(sums, "x", 2, 4)
    errors = sums / (full_len * model_width)
    reference_pair = ref_errors[0]
    margin = errors[0] - reference_pair[0] - (errors[1] - reference_pair[1])
    pair_loss = jax.nn.softplus(preference_beta * margin)
    weight_pair = (
        preference_beta
        * jax.nn.sigmoid(preference_beta * margin)
        * 2.0
        * LOSS_SCALE
        / (full_len * model_width)
    )
    image_scale = jnp.array([1.0, -1.0], f32) * weight_pair

    position = jnp.stack([z, dp]).astype(jnp.int32)
    grad_out = gradient(
        grad_out_kernel, "grad_out", position, image_scale, (residual, attended), ()
    )
    out_share = reduce_y(grad_out, dp, y_hi)
    grad_value = gradient(
        grad_value_kernel, "grad_value", position, image_scale, (residual, normed, probs), (out_w,)
    )
    value_share = reduce_y(grad_value, dp, y_hi)
    summed = reduce_z(jnp.stack([value_share, out_share]), z)
    return summed[0], summed[1].T, pair_loss.reshape(1)


def solution(mesh):
    fine = Mesh(mesh.devices.reshape(2, NZ, 2, 4, 2), ("dp", "z", "yh", "x", "core"))
    fsdp = ("z", "yh")
    in_specs = (
        P(GROUP, SEQ, None, None),
        P(GROUP, SEQ, None, None),
        P(GROUP, None),
        P(GROUP, None),
        P(),
        P(fsdp, SEQ),
        P(fsdp, SEQ),
        P(fsdp, SEQ),
        P(SEQ, fsdp),
    )
    out_specs = (P(GROUP, SEQ), P(SEQ, GROUP), P(GROUP))
    return jax.shard_map(body, mesh=fine, in_specs=in_specs, out_specs=out_specs, check_vma=False)
```

time: 351 us -> 283 us (0.81); the launches traced: 345 us -> 282 us
  starting transfers between devices: 107 us -> 53.7 us
  Pallas kernels: 0 us -> 37.7 us
  matrix products: 36.5 us -> 0 us
  waiting for transfers between devices: 137 us -> 157 us
  other arithmetic: 25.6 us -> 8.91 us
  local copies, waits for them, and re-layouts: 19.7 us -> 6.51 us
    pallas_call x0 -> x3, Pallas kernels: none -> 37.7 us  [the longest x2 19.9 us: gradient(): pl.pallas_call(kernel, grid=(2,), in_specs=[smem, smem] + [image_spec(a)...]
    ppermute x30 -> x15, starting transfers between devices: 62.9 us -> 28 us  [shift(): lax.ppermute(value, axis, [(i, (i + step) % count) for i in range(count)])]
    dot_general x10 -> x0, matrix products: 32 us -> none  [the longest x2 13.9 us: body(): qkv = jnp.dot(rows, weight, preferred_element_type=f32).astype(bf16)]
    ppermute x27 -> x20, waiting for transfers between devices: 29.3 us -> 50 us  [flip(): return lax.ppermute(value, axis, [(i, i ^ mask) for i in range(count)])]
    ppermute x27 -> x20, starting transfers between devices: 43.8 us -> 25.6 us  [flip(): return lax.ppermute(value, axis, [(i, i ^ mask) for i in range(count)])]
    unnamed x96 -> x50, local copies, waits for them, and re-layouts: 13.9 us -> 0.11 us
    concatenate x2 -> x1, other arithmetic: 5.09 us -> 0.09 us  [rolled(): twice = jnp.concatenate([value, value], axis=axis)]
    sub x2 -> x0, matrix products: 4.42 us -> none  [body(): prob = jax.nn.softmax(scores, axis=-1).astype(bf16)]
  transfers between devices with their start and end apart: 60 -> 38, of which waited for: 25 -> 27; matrix products, arithmetic and copies ran while one was open for 7% -> 2% of each run, Pallas kernels for 0% -> 2%
where the time goes in v2:
time: 283 us; the launch traced here: 282 us
  waiting for transfers between devices  157 us (55%)
  starting transfers between devices  53.7 us (19%)
  Pallas kernels  37.7 us (13%)
  between operations  18.3 us (6%)
  other arithmetic  8.91 us (3%)
  local copies, waits for them, and re-layouts  6.51 us (2%)
    ppermute x20, waiting for transfers between devices, flip(): return lax.ppermute(value, axis, [(i, i ^ mask) for i in range(count)])  50 us
    reduce_scatter x1, waiting for transfers between devices, body(): lax.psum_scatter(partial, SEQ, scatter_dimension=1, tiled=True).astype(f32)  44.5 us
    ppermute x15, waiting for transfers between devices, shift(): lax.ppermute(value, axis, [(i, (i + step) % count) for i in range(count)])  33.9 us
    all_gather x1, waiting for transfers between devices, body(): residual = lax.all_gather(differ.astype(bf16), SEQ, axis=1, tiled=True)  28.5 us
    ppermute x15, starting transfers between devices, shift(): lax.ppermute(value, axis, [(i, (i + step) % count) for i in range(count)])  28 us
    ppermute x20, starting transfers between devices, flip(): return lax.ppermute(value, axis, [(i, i ^ mask) for i in range(count)])  25.6 us
    pallas_call x2, Pallas kernels, gradient(): pl.pallas_call(kernel, grid=(2,), in_specs=[smem, smem] + [image_spec(a)...  19.9 us
    pallas_call x1, Pallas kernels, forward(): pl.pallas_call(functools.partial(forward_kernel, places, len(arrays)), gr...  17.8 us
  transfers between devices with their start and end apart: 38, of which 27 were waited for; matrix products, arithmetic and copies ran while one was open for 2% of the time, Pallas kernels for 2%

profile of v2, /device:TPU:32, one launch (start us, length us, event | category | flops | bytes accessed | tf_op | source)
XLA Modules:
  0.0 282.2 jit_solution(13019215779770099308)
XLA Ops:
  8.5 1.7 copy_bitcast_fusion
  13.0 3.1 %collective-permute-start = (bf16[192,512]{1,0:T(8,128)(2,1)S(1)}, bf16[192,512]{1,0:T(8,128)(2,1)S(1)}, u32[]{:S(2)}, u32[]{:S(2)}) collective-permute-start(bf16[192,512]{1,0:T(8,128)(2,1)S(1)} %pad_maximum_fusion.10), channel_id=1, source_target_pairs={{0,136},{8,128},{128,8},{136,0},{1,137},{9,129},{129,9},{137,1},{2... | collective-permute-start | bytes 589832 | tf_op jit(solution)/shard_map/ppermute | solution.py:31
  16.2 4.9 %collective-permute-done = bf16[192,512]{1,0:T(8,128)(2,1)S(1)} collective-permute-done((bf16[192,512]{1,0:T(8,128)(2,1)S(1)}, bf16[192,512]{1,0:T(8,128)(2,1)S(1)}, u32[]{:S(2)}, u32[]{:S(2)}) %collective-permute-start) | collective-permute-done | bytes 196640 | tf_op jit(solution)/shard_map/ppermute | solution.py:31
  21.1 2.0 collective-permute-start.4
  23.2 8.0 %collective-permute-done.4.refs_8_ = bf16[2,192,512]{2,1,0:T(8,128)(2,1)S(1)} collective-permute-done((bf16[2,192,512]{2,1,0:T(8,128)(2,1)S(1)}, bf16[2,192,512]{2,1,0:T(8,128)(2,1)S(1)}, u32[]{:S(2)}, u32[]{:S(2)}) %collective-permute-start.4) | collective-permute-done | bytes 393248 | tf_op jit(solution)/shard_map/ppermute | solution.py:27
  31.2 1.9 collective-permute-start.5
  33.2 2.4 collective-permute-start.2
  35.7 3.0 %collective-permute-start.10 = (bf16[3,192,512]{2,1,0:T(8,128)(2,1)S(1)}, bf16[3,192,512]{2,1,0:T(8,128)(2,1)S(1)}, u32[]{:S(2)}, u32[]{:S(2)}) collective-permute-start(bf16[3,192,512]{2,1,0:T(8,128)(2,1)S(1)} %pad_maximum_fusion.1), channel_id=1, source_target_pairs={{0,136},{8,128},{128,8},{136,0},{1,137},{9,129},{129,9},{137,1},{2... | collective-permute-start | bytes 1769480 | tf_op jit(solution)/shard_map/ppermute | solution.py:31
  38.9 4.4 %collective-permute-done.5.refs_7_ = bf16[2,192,512]{2,1,0:T(8,128)(2,1)S(1)} collective-permute-done((bf16[2,192,512]{2,1,0:T(8,128)(2,1)S(1)}, bf16[2,192,512]{2,1,0:T(8,128)(2,1)S(1)}, u32[]{:S(2)}, u32[]{:S(2)}) %collective-permute-start.5) | collective-permute-done | bytes 393248 | tf_op jit(solution)/shard_map/ppermute | solution.py:27
  43.7 2.6 collective-permute-start.3
  46.6 6.5 %collective-permute-done.6.refs_6_ = bf16[2,192,512]{2,1,0:T(8,128)(2,1)S(1)} collective-permute-done((bf16[2,192,512]{2,1,0:T(8,128)(2,1)S(1)}, bf16[2,192,512]{2,1,0:T(8,128)(2,1)S(1)}, u32[]{:S(2)}, u32[]{:S(2)}) %collective-permute-start.6) | collective-permute-done | bytes 393248 | tf_op jit(solution)/shard_map/ppermute | solution.py:27
  53.2 2.7 collective-permute-start.12
  56.4 2.8 collective-permute-start.14
  59.2 4.4 %collective-permute-done.11.refs_11_ = bf16[2,192,512]{2,1,0:T(8,128)(2,1)S(1)} collective-permute-done((bf16[2,192,512]{2,1,0:T(8,128)(2,1)S(1)}, bf16[2,192,512]{2,1,0:T(8,128)(2,1)S(1)}, u32[]{:S(2)}, u32[]{:S(2)}) %collective-permute-start.11) | collective-permute-done | bytes 393248 | tf_op jit(solution)/shard_map/ppermute | solution.py:31
  63.5 3.1 %collective-permute-start.8 = (bf16[1,192,512]{2,1,0:T(8,128)(2,1)S(1)}, bf16[1,192,512]{2,1,0:T(8,128)(2,1)S(1)}, u32[]{:S(2)}, u32[]{:S(2)}) collective-permute-start(bf16[1,192,512]{2,1,0:T(8,128)(2,1)S(1)} %get-tuple-element.39), channel_id=1, source_target_pairs={{0,112},{16,0},{32,16},{48,32},{64,48},{80,64},{96,80},{112,96},{1... | collective-permute-start | bytes 589832 | tf_op jit(solution)/shard_map/ppermute | solution.py:27
  66.7 3.2 %collective-permute-done.8.refs_5_ = bf16[1,192,512]{2,1,0:T(8,128)(2,1)S(1)} collective-permute-done((bf16[1,192,512]{2,1,0:T(8,128)(2,1)S(1)}, bf16[1,192,512]{2,1,0:T(8,128)(2,1)S(1)}, u32[]{:S(2)}, u32[]{:S(2)}) %collective-permute-start.8) | collective-permute-done | bytes 196640 | tf_op jit(solution)/shard_map/ppermute | solution.py:27
  70.9 2.1 collective-permute-done.14.refs_14_
  73.1 3.8 %collective-permute-done.16.refs_16_ = bf16[1,192,512]{2,1,0:T(8,128)(2,1)} collective-permute-done((bf16[1,192,512]{2,1,0:T(8,128)(2,1)S(1)}, bf16[1,192,512]{2,1,0:T(8,128)(2,1)}, u32[]{:S(2)}, u32[]{:S(2)}) %collective-permute-start.16) | collective-permute-done | bytes 196640 | tf_op jit(solution)/shard_map/ppermute | solution.py:31
  76.9 17.8 %forward.1 = (bf16[2,512,256]{2,1,0:T(8,128)(2,1)}, bf16[2,2,512,512]{3,2,1,0:T(8,128)(2,1)}, bf16[2,512,3072]{2,1,0:T(8,128)(2,1)}, bf16[3072,256]{1,0:T(8,128)(2,1)}) custom-call(bf16[2,512,3072]{2,1,0:T(8,128)(2,1)} %all-gather.3.cloned.1.call-done.normed, bf16[2,192,512]{2,1,0:T(8,128)(2,1)} %copy-done.2, bf16[2,192,512]{2,1,0:T(8,128)(2,1)} %copy-done.4, ...), custom_call_target="tpu_custom_call" | custom-call | tf_op jit(solution)/shard_map/forward/pallas_call | solution.py:119
  94.8 44.5 %reduce-scatter.2.cloned.1.call-done = bf16[2,64,3072]{2,1,0:T(8,128)(2,1)} async-done(((bf16[2,512,3072]{2,1,0:T(8,128)(2,1)}), bf16[2,64,3072]{2,1,0:T(8,128)(2,1)}) %reduce-scatter.2.cloned.1.call-update) | async-done | bytes 786448 | tf_op jit(solution)/shard_map/reduce_scatter | solution.py:261
  139.4 2.5 fusion.7
  144.5 3.4 %collective-permute-done.18 = f32[2]{0:T(128)S(1)} collective-permute-done((f32[2]{0:T(128)S(1)}, f32[2]{0:T(128)S(1)}, u32[]{:S(2)}, u32[]{:S(2)}) %collective-permute-start.18) | collective-permute-done | bytes 40 | tf_op jit(solution)/shard_map/ppermute | solution.py:31
  147.9 1.4 collective-permute-start.19
  149.3 3.7 %collective-permute-done.19 = f32[2]{0:T(128)S(1)} collective-permute-done((f32[2]{0:T(128)S(1)}, f32[2]{0:T(128)S(1)}, u32[]{:S(2)}, u32[]{:S(2)}) %collective-permute-start.19) | collective-permute-done | bytes 40 | tf_op jit(solution)/shard_map/ppermute | solution.py:31
  156.8 28.5 %all-gather.5.cloned.1.call-done.residual = bf16[2,512,3072]{2,1,0:T(8,128)(2,1)} async-done(((bf16[2,64,3072]{2,1,0:T(8,128)(2,1)}), bf16[2,512,3072]{2,1,0:T(8,128)(2,1)}) %all-gather.5.cloned.1.call-update) | async-done | bytes 6291472 | tf_op jit(solution)/shard_map/all_gather | solution.py:265
  185.3 13.9 %grad_value.1 = bf16[3072,256]{1,0:T(8,128)(2,1)} custom-call(s32[2]{0:T(128)} %pad_add_fusion.position, f32[2]{0:T(128)} %broadcast_multiply_fusion.scale, bf16[2,512,3072]{2,1,0:T(8,128)(2,1)} %all-gather.5.cloned.1.call-done.residual, bf16[2,512,3072]{2,1,0:T(8,128)(2,1)} %all-gather.3.cloned.1.call-done.normed, ...), custom_call_target="tpu_custom_call" | custom-call | tf_op jit(solution)/shard_map/grad_value/pallas_call | solution.py:193
  199.2 1.3 dynamic-slice_bitcast_fusion.14
  200.5 1.8 collective-permute-start.20
  202.3 6.0 %grad_out.1 = bf16[3072,256]{1,0:T(8,128)(2,1)} custom-call(s32[2]{0:T(128)} %pad_add_fusion.position, f32[2]{0:T(128)} %broadcast_multiply_fusion.scale, bf16[2,512,3072]{2,1,0:T(8,128)(2,1)} %all-gather.5.cloned.1.call-done.residual, bf16[2,512,256]{2,1,0:T(8,128)(2,1)} %get-tuple-element.10.attended), custom_call_target="tpu_custom_call" | custom-call | tf_op jit(solution)/shard_map/grad_out/pallas_call | solution.py:193
  210.3 2.8 %collective-permute-start.22 = (bf16[2,4,96,256]{3,2,1,0:T(8,128)(2,1)S(1)}, bf16[2,4,96,256]{3,2,1,0:T(8,128)(2,1)S(1)}, u32[]{:S(2)}, u32[]{:S(2)}) collective-permute-start(bf16[2,4,96,256]{3,2,1,0:T(8,128)(2,1)S(1)} %pad_maximum_fusion.7), channel_id=1, source_target_pairs={{0,136},{8,128},{128,8},{136,0},{1,137},{9,129},{129,9},{137,1},{2... | collective-permute-start | bytes 1179656 | tf_op jit(solution)/shard_map/ppermute | solution.py:31
  213.9 2.8 %collective-permute-start.21 = (bf16[4,96,256]{2,1,0:T(8,128)(2,1)S(1)}, bf16[4,96,256]{2,1,0:T(8,128)(2,1)S(1)}, u32[]{:S(2)}, u32[]{:S(2)}) collective-permute-start(bf16[4,96,256]{2,1,0:T(8,128)(2,1)S(1)} %fusion.26), channel_id=1, source_target_pairs={{0,136},{8,128},{128,8},{136,0},{1,137},{9,129},{129,9},{137,1},{2... | collective-permute-start | bytes 589832 | tf_op jit(solution)/shard_map/ppermute | solution.py:31
  216.8 4.0 %collective-permute-done.24 = bf16[2,4,96,256]{3,2,1,0:T(8,128)(2,1)S(1)} collective-permute-done((bf16[2,4,96,256]{3,2,1,0:T(8,128)(2,1)S(1)}, bf16[2,4,96,256]{3,2,1,0:T(8,128)(2,1)S(1)}, u32[]{:S(2)}, u32[]{:S(2)}) %collective-permute-start.24) | collective-permute-done | bytes 393248 | tf_op jit(solution)/shard_map/ppermute | solution.py:31
  220.9 2.7 collective-permute-start.25
  223.7 8.4 %collective-permute-done.26 = bf16[2,4,96,256]{3,2,1,0:T(8,128)(2,1)S(1)} collective-permute-done((bf16[2,4,96,256]{3,2,1,0:T(8,128)(2,1)S(1)}, bf16[2,4,96,256]{3,2,1,0:T(8,128)(2,1)S(1)}, u32[]{:S(2)}, u32[]{:S(2)}) %collective-permute-start.26) | collective-permute-done | bytes 393248 | tf_op jit(solution)/shard_map/ppermute | solution.py:31
  232.1 4.1 %collective-permute-done.21 = bf16[4,96,256]{2,1,0:T(8,128)(2,1)S(1)} collective-permute-done((bf16[4,96,256]{2,1,0:T(8,128)(2,1)S(1)}, bf16[4,96,256]{2,1,0:T(8,128)(2,1)S(1)}, u32[]{:S(2)}, u32[]{:S(2)}) %collective-permute-start.21) | collective-permute-done | bytes 196640 | tf_op jit(solution)/shard_map/ppermute | solution.py:31
  236.8 2.4 collective-permute-done.25
  239.7 3.9 %collective-permute-done.23 = bf16[4,96,256]{2,1,0:T(8,128)(2,1)S(1)} collective-permute-done((bf16[4,96,256]{2,1,0:T(8,128)(2,1)S(1)}, bf16[4,96,256]{2,1,0:T(8,128)(2,1)S(1)}, u32[]{:S(2)}, u32[]{:S(2)}) %collective-permute-start.23) | collective-permute-done | bytes 196640 | tf_op jit(solution)/shard_map/ppermute | solution.py:31
  243.6 2.7 collective-permute-done.27
  246.6 1.6 collective-permute-start.28
  248.2 3.8 %collective-permute-start.29 = (bf16[2,96,256]{2,1,0:T(8,128)(2,1)S(1)}, bf16[2,96,256]{2,1,0:T(8,128)(2,1)S(1)}, u32[]{:S(2)}, u32[]{:S(2)}) collective-permute-start(bf16[2,96,256]{2,1,0:T(8,128)(2,1)S(1)} %get-tuple-element.35), channel_id=1, source_target_pairs={{0,32},{16,48},{32,64},{48,80},{64,96},{80,112},{96,0},{112,16},{1... | collective-permute-start | bytes 294920 | tf_op jit(solution)/shard_map/ppermute | solution.py:27
  252.8 2.9 %collective-permute-start.31 = (bf16[2,96,256]{2,1,0:T(8,128)(2,1)S(1)}, bf16[2,96,256]{2,1,0:T(8,128)(2,1)S(1)}, u32[]{:S(2)}, u32[]{:S(2)}) collective-permute-start(bf16[2,96,256]{2,1,0:T(8,128)(2,1)S(1)} %get-tuple-element.33), channel_id=1, source_target_pairs={{0,64},{16,80},{32,96},{48,112},{64,0},{80,16},{96,32},{112,48},{1... | collective-permute-start | bytes 294920 | tf_op jit(solution)/shard_map/ppermute | solution.py:27
  255.7 1.7 collective-permute-start.32
  257.4 2.7 collective-permute-start.33
  260.5 2.2 collective-permute-start.34
  262.8 3.5 %collective-permute-done.30 = bf16[2,96,256]{2,1,0:T(8,128)(2,1)S(1)} collective-permute-done((bf16[2,96,256]{2,1,0:T(8,128)(2,1)S(1)}, bf16[2,96,256]{2,1,0:T(8,128)(2,1)S(1)}, u32[]{:S(2)}, u32[]{:S(2)}) %collective-permute-start.30) | collective-permute-done | bytes 98336 | tf_op jit(solution)/shard_map/ppermute | solution.py:27
  266.3 3.9 %collective-permute-done.32 = bf16[2,96,256]{2,1,0:T(8,128)(2,1)S(1)} collective-permute-done((bf16[2,96,256]{2,1,0:T(8,128)(2,1)S(1)}, bf16[2,96,256]{2,1,0:T(8,128)(2,1)S(1)}, u32[]{:S(2)}, u32[]{:S(2)}) %collective-permute-start.32) | collective-permute-done | bytes 98336 | tf_op jit(solution)/shard_map/ppermute | solution.py:27
  270.2 2.2 collective-permute-done.33
  272.4 1.4 collective-permute-done.34
  (137 shorter events, 16.8 us)
Async XLA Ops:
  7.2 69.7 %all-gather.3.cloned.1.call-start = ((), (), s32[]{:S(2)}) async-start(), calls=%async_computation.1 | async-start | bytes 7077888 | tf_op jit(solution)/shard_map/all_gather | solution.py:259
  12.8 126.5 %reduce-scatter.2.cloned.1.call-start = ((), (), s32[]{:S(2)}) async-start(), calls=%async_computation.2 | async-start | bytes 7077888 | tf_op jit(solution)/shard_map/reduce_scatter | solution.py:261
  13.0 8.0 %collective-permute-start = (bf16[192,512]{1,0:T(8,128)(2,1)S(1)}, bf16[192,512]{1,0:T(8,128)(2,1)S(1)}, u32[]{:S(2)}, u32[]{:S(2)}) collective-permute-start(bf16[192,512]{1,0:T(8,128)(2,1)S(1)} %pad_maximum_fusion.10), channel_id=1, source_target_pairs={{0,136},{8,128},{128,8},{136,0},{1,137},{9,129},{129,9},{137,1},{2... | collective-permute-start | bytes 589832 | tf_op jit(solution)/shard_map/ppermute | solution.py:31
  21.1 14.6 %copy-start.2 = (bf16[2,192,512]{2,1,0:T(8,128)(2,1)}, bf16[2,192,512]{2,1,0:T(8,128)(2,1)S(1)}, u32[]{:S(2)}) copy-start(bf16[2,192,512]{2,1,0:T(8,128)(2,1)S(1)} %maximum_select_fusion.refs_0_) | copy-start | bytes 1179652
  21.1 10.1 %collective-permute-start.4 = (bf16[2,192,512]{2,1,0:T(8,128)(2,1)S(1)}, bf16[2,192,512]{2,1,0:T(8,128)(2,1)S(1)}, u32[]{:S(2)}, u32[]{:S(2)}) collective-permute-start(bf16[2,192,512]{2,1,0:T(8,128)(2,1)S(1)} %maximum_select_fusion.refs_0_), channel_id=1, source_target_pairs={{0,16},{16,32},{32,48},{48,64},{64,80},{80,96},{96,112},{112,0},{1... | collective-permute-start | bytes 1179656 | tf_op jit(solution)/shard_map/ppermute | solution.py:27
  23.1 10.1 %collective-permute-start.1 = (bf16[2,192,512]{2,1,0:T(8,128)(2,1)S(1)}, bf16[2,192,512]{2,1,0:T(8,128)(2,1)S(1)}, u32[]{:S(2)}, u32[]{:S(2)}) collective-permute-start(bf16[2,192,512]{2,1,0:T(8,128)(2,1)S(1)} %maximum_select_fusion.refs_0_), channel_id=1, source_target_pairs={{0,112},{16,0},{32,16},{48,32},{64,48},{80,64},{96,80},{112,96},{1... | collective-permute-start | bytes 1179656 | tf_op jit(solution)/shard_map/ppermute | solution.py:27
  31.2 7.5 %copy-start.3 = (bf16[2,192,512]{2,1,0:T(8,128)(2,1)}, bf16[2,192,512]{2,1,0:T(8,128)(2,1)S(1)}, u32[]{:S(2)}) copy-start(bf16[2,192,512]{2,1,0:T(8,128)(2,1)S(1)} %collective-permute-done.4.refs_8_) | copy-start | bytes 1179652
  31.2 12.0 %collective-permute-start.5 = (bf16[2,192,512]{2,1,0:T(8,128)(2,1)S(1)}, bf16[2,192,512]{2,1,0:T(8,128)(2,1)S(1)}, u32[]{:S(2)}, u32[]{:S(2)}) collective-permute-start(bf16[2,192,512]{2,1,0:T(8,128)(2,1)S(1)} %collective-permute-done.4.refs_8_), channel_id=1, source_target_pairs={{0,16},{16,32},{32,48},{48,64},{64,80},{80,96},{96,112},{112,0},{1... | collective-permute-start | bytes 1179656 | tf_op jit(solution)/shard_map/ppermute | solution.py:27
  33.2 10.5 %collective-permute-start.2 = (bf16[2,192,512]{2,1,0:T(8,128)(2,1)S(1)}, bf16[2,192,512]{2,1,0:T(8,128)(2,1)S(1)}, u32[]{:S(2)}, u32[]{:S(2)}) collective-permute-start(bf16[2,192,512]{2,1,0:T(8,128)(2,1)S(1)} %collective-permute-done.1.refs_1_), channel_id=1, source_target_pairs={{0,112},{16,0},{32,16},{48,32},{64,48},{80,64},{96,80},{112,96},{1... | collective-permute-start | bytes 1179656 | tf_op jit(solution)/shard_map/ppermute | solution.py:27
  35.7 20.5 %collective-permute-start.10 = (bf16[3,192,512]{2,1,0:T(8,128)(2,1)S(1)}, bf16[3,192,512]{2,1,0:T(8,128)(2,1)S(1)}, u32[]{:S(2)}, u32[]{:S(2)}) collective-permute-start(bf16[3,192,512]{2,1,0:T(8,128)(2,1)S(1)} %pad_maximum_fusion.1), channel_id=1, source_target_pairs={{0,136},{8,128},{128,8},{136,0},{1,137},{9,129},{129,9},{137,1},{2... | collective-permute-start | bytes 1769480 | tf_op jit(solution)/shard_map/ppermute | solution.py:31
  38.8 17.6 %collective-permute-start.9 = (bf16[3,192,512]{2,1,0:T(8,128)(2,1)S(1)}, bf16[3,192,512]{2,1,0:T(8,128)(2,1)S(1)}, u32[]{:S(2)}, u32[]{:S(2)}) collective-permute-start(bf16[3,192,512]{2,1,0:T(8,128)(2,1)S(1)} %pad_maximum_fusion), channel_id=1, source_target_pairs={{0,128},{8,136},{128,0},{136,8},{1,129},{9,137},{129,1},{137,9},{2... | collective-permute-start | bytes 1769480 | tf_op jit(solution)/shard_map/ppermute | solution.py:31
  43.2 9.9 %collective-permute-start.6 = (bf16[2,192,512]{2,1,0:T(8,128)(2,1)S(1)}, bf16[2,192,512]{2,1,0:T(8,128)(2,1)S(1)}, u32[]{:S(2)}, u32[]{:S(2)}) collective-permute-start(bf16[2,192,512]{2,1,0:T(8,128)(2,1)S(1)} %collective-permute-done.5.refs_7_), channel_id=1, source_target_pairs={{0,16},{16,32},{32,48},{48,64},{64,80},{80,96},{96,112},{112,0},{1... | collective-permute-start | bytes 1179656 | tf_op jit(solution)/shard_map/ppermute | solution.py:27
  43.7 12.2 %collective-permute-start.3 = (bf16[2,192,512]{2,1,0:T(8,128)(2,1)S(1)}, bf16[2,192,512]{2,1,0:T(8,128)(2,1)S(1)}, u32[]{:S(2)}, u32[]{:S(2)}) collective-permute-start(bf16[2,192,512]{2,1,0:T(8,128)(2,1)S(1)} %collective-permute-done.2.refs_2_), channel_id=1, source_target_pairs={{0,112},{16,0},{32,16},{48,32},{64,48},{80,64},{96,80},{112,96},{1... | collective-permute-start | bytes 1179656 | tf_op jit(solution)/shard_map/ppermute | solution.py:27
  46.4 17.1 %collective-permute-start.11 = (bf16[2,192,512]{2,1,0:T(8,128)(2,1)S(1)}, bf16[2,192,512]{2,1,0:T(8,128)(2,1)S(1)}, u32[]{:S(2)}, u32[]{:S(2)}) collective-permute-start(bf16[2,192,512]{2,1,0:T(8,128)(2,1)S(1)} %pad_maximum_fusion.2), channel_id=1, source_target_pairs={{0,128},{8,136},{128,0},{136,8},{1,129},{9,137},{129,1},{137,9},{2... | collective-permute-start | bytes 1179656 | tf_op jit(solution)/shard_map/ppermute | solution.py:31
  53.2 16.8 %collective-permute-start.12 = (bf16[2,192,512]{2,1,0:T(8,128)(2,1)S(1)}, bf16[2,192,512]{2,1,0:T(8,128)(2,1)S(1)}, u32[]{:S(2)}, u32[]{:S(2)}) collective-permute-start(bf16[2,192,512]{2,1,0:T(8,128)(2,1)S(1)} %pad_maximum_fusion.3), channel_id=1, source_target_pairs={{0,136},{8,128},{128,8},{136,0},{1,137},{9,129},{129,9},{137,1},{2... | collective-permute-start | bytes 1179656 | tf_op jit(solution)/shard_map/ppermute | solution.py:31
  55.9 20.9 %copy-start.8 = (bf16[2,192,512]{2,1,0:T(8,128)(2,1)}, bf16[2,192,512]{2,1,0:T(8,128)(2,1)S(1)}, u32[]{:S(2)}) copy-start(bf16[2,192,512]{2,1,0:T(8,128)(2,1)S(1)} %collective-permute-done.3.refs_3_) | copy-start | bytes 1179652
  55.9 10.8 %collective-permute-start.7 = (bf16[1,192,512]{2,1,0:T(8,128)(2,1)S(1)}, bf16[1,192,512]{2,1,0:T(8,128)(2,1)S(1)}, u32[]{:S(2)}, u32[]{:S(2)}) collective-permute-start(bf16[1,192,512]{2,1,0:T(8,128)(2,1)S(1)} %get-tuple-element.37), channel_id=1, source_target_pairs={{0,16},{16,32},{32,48},{48,64},{64,80},{80,96},{96,112},{112,0},{1... | collective-permute-start | bytes 589832 | tf_op jit(solution)/shard_map/ppermute | solution.py:27
  56.2 13.7 %copy-start.9 = (bf16[3,192,512]{2,1,0:T(8,128)(2,1)}, bf16[3,192,512]{2,1,0:T(8,128)(2,1)S(1)}, u32[]{:S(2)}) copy-start(bf16[3,192,512]{2,1,0:T(8,128)(2,1)S(1)} %collective-permute-done.10.refs_10_) | copy-start | bytes 1769476
  56.2 14.7 %collective-permute-start.13 = (bf16[2,192,512]{2,1,0:T(8,128)(2,1)S(1)}, bf16[2,192,512]{2,1,0:T(8,128)(2,1)S(1)}, u32[]{:S(2)}, u32[]{:S(2)}) collective-permute-start(bf16[2,192,512]{2,1,0:T(8,128)(2,1)S(1)} %pad_maximum_fusion.4), channel_id=1, source_target_pairs={{0,128},{8,136},{128,0},{136,8},{1,129},{9,137},{129,1},{137,9},{2... | collective-permute-start | bytes 1179656 | tf_op jit(solution)/shard_map/ppermute | solution.py:31
  56.4 13.6 %copy-start.10 = (bf16[3,192,512]{2,1,0:T(8,128)(2,1)}, bf16[3,192,512]{2,1,0:T(8,128)(2,1)S(1)}, u32[]{:S(2)}) copy-start(bf16[3,192,512]{2,1,0:T(8,128)(2,1)S(1)} %collective-permute-done.9.refs_9_) | copy-start | bytes 1769476
  56.4 16.7 %collective-permute-start.14 = (bf16[2,192,512]{2,1,0:T(8,128)(2,1)S(1)}, bf16[2,192,512]{2,1,0:T(8,128)(2,1)S(1)}, u32[]{:S(2)}, u32[]{:S(2)}) collective-permute-start(bf16[2,192,512]{2,1,0:T(8,128)(2,1)S(1)} %pad_maximum_fusion.5), channel_id=1, source_target_pairs={{0,136},{8,128},{128,8},{136,0},{1,137},{9,129},{129,9},{137,1},{2... | collective-permute-start | bytes 1179656 | tf_op jit(solution)/shard_map/ppermute | solution.py:31
  63.5 6.4 %copy-start.11 = (bf16[2,192,512]{2,1,0:T(8,128)(2,1)}, bf16[2,192,512]{2,1,0:T(8,128)(2,1)S(1)}, u32[]{:S(2)}) copy-start(bf16[2,192,512]{2,1,0:T(8,128)(2,1)S(1)} %collective-permute-done.11.refs_11_) | copy-start | bytes 1179652
  63.5 6.3 %collective-permute-start.8 = (bf16[1,192,512]{2,1,0:T(8,128)(2,1)S(1)}, bf16[1,192,512]{2,1,0:T(8,128)(2,1)S(1)}, u32[]{:S(2)}, u32[]{:S(2)}) collective-permute-start(bf16[1,192,512]{2,1,0:T(8,128)(2,1)S(1)} %get-tuple-element.39), channel_id=1, source_target_pairs={{0,112},{16,0},{32,16},{48,32},{64,48},{80,64},{96,80},{112,96},{1... | collective-permute-start | bytes 589832 | tf_op jit(solution)/shard_map/ppermute | solution.py:27
  66.7 6.4 %collective-permute-start.15 = (bf16[1,192,512]{2,1,0:T(8,128)(2,1)S(1)}, bf16[1,192,512]{2,1,0:T(8,128)(2,1)S(1)}, u32[]{:S(2)}, u32[]{:S(2)}) collective-permute-start(bf16[1,192,512]{2,1,0:T(8,128)(2,1)S(1)} %collective-permute-done.7.refs_4_), channel_id=1, source_target_pairs={{0,128},{8,136},{128,0},{136,8},{1,129},{9,137},{129,1},{137,9},{2... | collective-permute-start | bytes 589832 | tf_op jit(solution)/shard_map/ppermute | solution.py:31
  69.9 7.0 %copy-start.16 = (bf16[1,192,512]{2,1,0:T(8,128)(2,1)}, bf16[1,192,512]{2,1,0:T(8,128)(2,1)S(1)}, u32[]{:S(2)}) copy-start(bf16[1,192,512]{2,1,0:T(8,128)(2,1)S(1)} %collective-permute-done.8.refs_5_) | copy-start | bytes 589828
  69.9 7.0 %collective-permute-start.16 = (bf16[1,192,512]{2,1,0:T(8,128)(2,1)S(1)}, bf16[1,192,512]{2,1,0:T(8,128)(2,1)}, u32[]{:S(2)}, u32[]{:S(2)}) collective-permute-start(bf16[1,192,512]{2,1,0:T(8,128)(2,1)S(1)} %collective-permute-done.8.refs_5_), channel_id=1, source_target_pairs={{0,136},{8,128},{128,8},{136,0},{1,137},{9,129},{129,9},{137,1},{2... | collective-permute-start | bytes 589832 | tf_op jit(solution)/shard_map/ppermute | solution.py:31
  70.0 6.9 %copy-start.12 = (bf16[2,192,512]{2,1,0:T(8,128)(2,1)}, bf16[2,192,512]{2,1,0:T(8,128)(2,1)S(1)}, u32[]{:S(2)}) copy-start(bf16[2,192,512]{2,1,0:T(8,128)(2,1)S(1)} %collective-permute-done.12.refs_12_) | copy-start | bytes 1179652
  94.8 90.5 %all-gather.5.cloned.1.call-start = ((), (), s32[]{:S(2)}) async-start(), calls=%async_computation.3 | async-start | bytes 7077888 | tf_op jit(solution)/shard_map/all_gather | solution.py:265
  139.4 16.9 %copy-start.24 = (f32[2]{0:T(128)S(1)}, f32[2]{0:T(128)}, u32[]{:S(2)}) copy-start(f32[2]{0:T(128)} %constant.382.clone) | copy-start | bytes 28
  143.3 1.1 collective-permute-start.17
  144.4 3.5 %collective-permute-start.18 = (f32[2]{0:T(128)S(1)}, f32[2]{0:T(128)S(1)}, u32[]{:S(2)}, u32[]{:S(2)}) collective-permute-start(f32[2]{0:T(128)S(1)} %add.264), channel_id=1, source_target_pairs={{0,2},{2,0},{4,6},{6,4},{1,3},{3,1},{5,7},{7,5},{8,10},{10,8},{12,... | collective-permute-start | bytes 32 | tf_op jit(solution)/shard_map/ppermute | solution.py:31
  147.9 5.0 %collective-permute-start.19 = (f32[2]{0:T(128)S(1)}, f32[2]{0:T(128)S(1)}, u32[]{:S(2)}, u32[]{:S(2)}) collective-permute-start(f32[2]{0:T(128)S(1)} %add.265), channel_id=1, source_target_pairs={{0,4},{2,6},{4,0},{6,2},{1,5},{3,7},{5,1},{7,3},{8,12},{10,14},{12... | collective-permute-start | bytes 32 | tf_op jit(solution)/shard_map/ppermute | solution.py:31
  200.5 13.2 %collective-permute-start.20 = (bf16[2,4,96,256]{3,2,1,0:T(8,128)(2,1)S(1)}, bf16[2,4,96,256]{3,2,1,0:T(8,128)(2,1)S(1)}, u32[]{:S(2)}, u32[]{:S(2)}) collective-permute-start(bf16[2,4,96,256]{3,2,1,0:T(8,128)(2,1)S(1)} %pad_maximum_fusion.6), channel_id=1, source_target_pairs={{0,128},{8,136},{128,0},{136,8},{1,129},{9,137},{129,1},{137,9},{2... | collective-permute-start | bytes 1179656 | tf_op jit(solution)/shard_map/ppermute | solution.py:31
  209.7 11.1 %collective-permute-start.24 = (bf16[2,4,96,256]{3,2,1,0:T(8,128)(2,1)S(1)}, bf16[2,4,96,256]{3,2,1,0:T(8,128)(2,1)S(1)}, u32[]{:S(2)}, u32[]{:S(2)}) collective-permute-start(bf16[2,4,96,256]{3,2,1,0:T(8,128)(2,1)S(1)} %pad_maximum_fusion.8), channel_id=1, source_target_pairs={{0,128},{8,136},{128,0},{136,8},{1,129},{9,137},{129,1},{137,9},{2... | collective-permute-start | bytes 1179656 | tf_op jit(solution)/shard_map/ppermute | solution.py:31
  210.3 13.3 %collective-permute-start.22 = (bf16[2,4,96,256]{3,2,1,0:T(8,128)(2,1)S(1)}, bf16[2,4,96,256]{3,2,1,0:T(8,128)(2,1)S(1)}, u32[]{:S(2)}, u32[]{:S(2)}) collective-permute-start(bf16[2,4,96,256]{3,2,1,0:T(8,128)(2,1)S(1)} %pad_maximum_fusion.7), channel_id=1, source_target_pairs={{0,136},{8,128},{128,8},{136,0},{1,137},{9,129},{129,9},{137,1},{2... | collective-permute-start | bytes 1179656 | tf_op jit(solution)/shard_map/ppermute | solution.py:31
  213.2 7.6 %copy-start.1 = (bf16[3072,256]{1,0:T(8,128)(2,1)S(1)}, bf16[3072,256]{1,0:T(8,128)(2,1)}, u32[]{:S(2)}) copy-start(bf16[3072,256]{1,0:T(8,128)(2,1)} %grad_out.1) | copy-start | bytes 4718596
  213.2 18.9 %collective-permute-start.26 = (bf16[2,4,96,256]{3,2,1,0:T(8,128)(2,1)S(1)}, bf16[2,4,96,256]{3,2,1,0:T(8,128)(2,1)S(1)}, u32[]{:S(2)}, u32[]{:S(2)}) collective-permute-start(bf16[2,4,96,256]{3,2,1,0:T(8,128)(2,1)S(1)} %pad_maximum_fusion.9), channel_id=1, source_target_pairs={{0,136},{8,128},{128,8},{136,0},{1,137},{9,129},{129,9},{137,1},{2... | collective-permute-start | bytes 1179656 | tf_op jit(solution)/shard_map/ppermute | solution.py:31
  213.9 22.4 %collective-permute-start.21 = (bf16[4,96,256]{2,1,0:T(8,128)(2,1)S(1)}, bf16[4,96,256]{2,1,0:T(8,128)(2,1)S(1)}, u32[]{:S(2)}, u32[]{:S(2)}) collective-permute-start(bf16[4,96,256]{2,1,0:T(8,128)(2,1)S(1)} %fusion.26), channel_id=1, source_target_pairs={{0,136},{8,128},{128,8},{136,0},{1,137},{9,129},{129,9},{137,1},{2... | collective-permute-start | bytes 589832 | tf_op jit(solution)/shard_map/ppermute | solution.py:31
  220.9 18.3 %collective-permute-start.25 = (bf16[4,96,256]{2,1,0:T(8,128)(2,1)S(1)}, bf16[4,96,256]{2,1,0:T(8,128)(2,1)S(1)}, u32[]{:S(2)}, u32[]{:S(2)}) collective-permute-start(bf16[4,96,256]{2,1,0:T(8,128)(2,1)S(1)} %fusion.16), channel_id=1, source_target_pairs={{0,136},{8,128},{128,8},{136,0},{1,137},{9,129},{129,9},{137,1},{2... | collective-permute-start | bytes 589832 | tf_op jit(solution)/shard_map/ppermute | solution.py:31
  236.4 7.2 %collective-permute-start.23 = (bf16[4,96,256]{2,1,0:T(8,128)(2,1)S(1)}, bf16[4,96,256]{2,1,0:T(8,128)(2,1)S(1)}, u32[]{:S(2)}, u32[]{:S(2)}) collective-permute-start(bf16[4,96,256]{2,1,0:T(8,128)(2,1)S(1)} %get-tuple-element.18), channel_id=1, source_target_pairs={{0,128},{8,136},{128,0},{136,8},{1,129},{9,137},{129,1},{137,9},{2... | collective-permute-start | bytes 589832 | tf_op jit(solution)/shard_map/ppermute | solution.py:31
  239.3 7.1 %collective-permute-start.27 = (bf16[4,96,256]{2,1,0:T(8,128)(2,1)S(1)}, bf16[4,96,256]{2,1,0:T(8,128)(2,1)S(1)}, u32[]{:S(2)}, u32[]{:S(2)}) collective-permute-start(bf16[4,96,256]{2,1,0:T(8,128)(2,1)S(1)} %get-tuple-element.24), channel_id=1, source_target_pairs={{0,128},{8,136},{128,0},{136,8},{1,129},{9,137},{129,1},{137,9},{2... | collective-permute-start | bytes 589832 | tf_op jit(solution)/shard_map/ppermute | solution.py:31
  246.6 10.8 %collective-permute-start.28 = (bf16[2,96,256]{2,1,0:T(8,128)(2,1)S(1)}, bf16[2,96,256]{2,1,0:T(8,128)(2,1)S(1)}, u32[]{:S(2)}, u32[]{:S(2)}) collective-permute-start(bf16[2,96,256]{2,1,0:T(8,128)(2,1)S(1)} %get-tuple-element.29), channel_id=1, source_target_pairs={{0,16},{16,32},{32,48},{48,64},{64,80},{80,96},{96,112},{112,0},{1... | collective-permute-start | bytes 294920 | tf_op jit(solution)/shard_map/ppermute | solution.py:27
  248.2 12.3 %collective-permute-start.29 = (bf16[2,96,256]{2,1,0:T(8,128)(2,1)S(1)}, bf16[2,96,256]{2,1,0:T(8,128)(2,1)S(1)}, u32[]{:S(2)}, u32[]{:S(2)}) collective-permute-start(bf16[2,96,256]{2,1,0:T(8,128)(2,1)S(1)} %get-tuple-element.35), channel_id=1, source_target_pairs={{0,32},{16,48},{32,64},{48,80},{64,96},{80,112},{96,0},{112,16},{1... | collective-permute-start | bytes 294920 | tf_op jit(solution)/shard_map/ppermute | solution.py:27
  252.0 14.3 %collective-permute-start.30 = (bf16[2,96,256]{2,1,0:T(8,128)(2,1)S(1)}, bf16[2,96,256]{2,1,0:T(8,128)(2,1)S(1)}, u32[]{:S(2)}, u32[]{:S(2)}) collective-permute-start(bf16[2,96,256]{2,1,0:T(8,128)(2,1)S(1)} %get-tuple-element.34), channel_id=1, source_target_pairs={{0,48},{16,64},{32,80},{48,96},{64,112},{80,0},{96,16},{112,32},{1... | collective-permute-start | bytes 294920 | tf_op jit(solution)/shard_map/ppermute | solution.py:27
  252.8 13.5 %collective-permute-start.31 = (bf16[2,96,256]{2,1,0:T(8,128)(2,1)S(1)}, bf16[2,96,256]{2,1,0:T(8,128)(2,1)S(1)}, u32[]{:S(2)}, u32[]{:S(2)}) collective-permute-start(bf16[2,96,256]{2,1,0:T(8,128)(2,1)S(1)} %get-tuple-element.33), channel_id=1, source_target_pairs={{0,64},{16,80},{32,96},{48,112},{64,0},{80,16},{96,32},{112,48},{1... | collective-permute-start | bytes 294920 | tf_op jit(solution)/shard_map/ppermute | solution.py:27
  255.7 14.5 %collective-permute-start.32 = (bf16[2,96,256]{2,1,0:T(8,128)(2,1)S(1)}, bf16[2,96,256]{2,1,0:T(8,128)(2,1)S(1)}, u32[]{:S(2)}, u32[]{:S(2)}) collective-permute-start(bf16[2,96,256]{2,1,0:T(8,128)(2,1)S(1)} %get-tuple-element.32), channel_id=1, source_target_pairs={{0,80},{16,96},{32,112},{48,0},{64,16},{80,32},{96,48},{112,64},{1... | collective-permute-start | bytes 294920 | tf_op jit(solution)/shard_map/ppermute | solution.py:27
  257.4 15.0 %collective-permute-start.33 = (bf16[2,96,256]{2,1,0:T(8,128)(2,1)S(1)}, bf16[2,96,256]{2,1,0:T(8,128)(2,1)S(1)}, u32[]{:S(2)}, u32[]{:S(2)}) collective-permute-start(bf16[2,96,256]{2,1,0:T(8,128)(2,1)S(1)} %get-tuple-element.31), channel_id=1, source_target_pairs={{0,96},{16,112},{32,0},{48,16},{64,32},{80,48},{96,64},{112,80},{1... | collective-permute-start | bytes 294920 | tf_op jit(solution)/shard_map/ppermute | solution.py:27
  260.5 13.3 %collective-permute-start.34 = (bf16[2,96,256]{2,1,0:T(8,128)(2,1)S(1)}, bf16[2,96,256]{2,1,0:T(8,128)(2,1)S(1)}, u32[]{:S(2)}, u32[]{:S(2)}) collective-permute-start(bf16[2,96,256]{2,1,0:T(8,128)(2,1)S(1)} %get-tuple-element.30), channel_id=1, source_target_pairs={{0,112},{16,0},{32,16},{48,32},{64,48},{80,64},{96,80},{112,96},{1... | collective-permute-start | bytes 294920 | tf_op jit(solution)/shard_map/ppermute | solution.py:27
  (15 other events, 49.4 us)
Sparse Core Ops, SparseCore 0:
  13.0 46.0 all-gather.2
  94.9 44.4 reduce-scatter.1
  142.0 43.2 all-gather.4
